TPU v7x, 32 devices: a whole 2x2x4 slice. The times are simulated.
32 devices in a mesh: blk: 16 (over z, y, x), col: 2 (over core).
Axes of the slice: x: 2, y: 2, z: 4, core: 2. Of those that a mesh axis runs over, the one named last changes fastest.
Arguments:
- psi: bfloat16 [32, 384, 384], P('blk', 'col')
- dims: int32 [32], P('blk'), may hold values from 192 to 384, as said below
- pattern: int32 [32, 5], P('blk'), may hold values 0 or 1
- left_env: bfloat16 [32, 4, 384, 384], P('blk', 'col')
- right_env: bfloat16 [4, 384, 384], P('col')
Outputs:
- sigma_first: float32 [32, 384, 384], P('blk', 'col')
- sigma_second: float32 [32, 384, 384], P('blk', 'col')
Inputs may be any that keep to these rules, and one draw needn't show every extreme that they name: dims[s] lies between 192 and 384.
All inputs are finite; a program needn't handle non-finite values. No bound on the sum of `pattern` on one device may be relied on, other than what follows from the above.
Results may differ from a plain program's by a relative error of at most 0.022.
Values may be sent and summed in bfloat16 or wider, within the bound.
A program may use at most 64 MiB of HBM per device.

v0:
```python
import jax
import jax.numpy as jnp
from jax import lax
from jax.sharding import PartitionSpec as P

W_COL = 2


def with_halo(block, sides, width):
    for axis, dim in sides:
        count = lax.axis_size(axis)
        forward = [(i, i + 1) for i in range(count - 1)]
        backward = [(target, source) for source, target in forward]
        low = lax.ppermute(
            lax.slice_in_dim(block, block.shape[dim] - width, None, axis=dim), axis, forward
        )
        high = lax.ppermute(lax.slice_in_dim(block, 0, width, axis=dim), axis, backward)
        block = jnp.concatenate([low, block, high], axis=dim)
    return block


def combine_blocks(padded, pattern, sectors):
    coeff = pattern.astype(jnp.float32)
    total = jnp.zeros((sectors,) + padded.shape[1:], jnp.float32)
    for offset in range(pattern.shape[1]):
        total = total + coeff[:, offset, None, None] * padded[offset : offset + sectors].astype(
            jnp.float32
        )
    return total.astype(jnp.bfloat16)


def apply_hamiltonian(vector, pattern, left_env, right_env, mask, scale):
    sectors = vector.shape[0]
    full = lax.all_gather(vector, "col", axis=1, tiled=True)
    padded = with_halo(full, (("blk", 0),), 2)
    combined = combine_blocks(padded, pattern, sectors)
    temp = jnp.einsum(
        "swab,sbc->swac", left_env, combined, preferred_element_type=jnp.float32
    ).astype(jnp.bfloat16)
    partial_term = jnp.einsum("swac,wdc->sad", temp, right_env, preferred_element_type=jnp.float32)
    summed = lax.psum_scatter(
        partial_term.astype(jnp.bfloat16), "col", scatter_dimension=1, tiled=True
    ).astype(jnp.float32)
    return jnp.where(mask, summed * scale, jnp.float32(0.0))


def body(psi, dims, pattern, left_env, right_env):
    rows = psi.shape[1]
    width = psi.shape[2]
    row_ids = lax.axis_index("col") * rows + jnp.arange(rows, dtype=jnp.int32)
    col_ids = jnp.arange(width, dtype=jnp.int32)
    mask = (row_ids[None, :, None] < dims[:, None, None]) & (
        col_ids[None, None, :] < dims[:, None, None]
    )
    psi_m = jnp.where(mask, psi, jnp.zeros_like(psi))
    scale = 1.0 / jnp.sqrt(jnp.float32(W_COL * lax.axis_size("col")))
    sigma_first = apply_hamiltonian(psi_m, pattern, left_env, right_env, mask, scale)
    psi_float = psi_m.astype(jnp.float32)
    numerator, denominator = lax.psum(
        (jnp.sum(psi_float * sigma_first), jnp.sum(psi_float * psi_float)), ("blk", "col")
    )
    theta = numerator / denominator
    resid = (sigma_first - theta * psi_float).astype(jnp.bfloat16)
    sigma_second = apply_hamiltonian(resid, pattern, left_env, right_env, mask, scale)
    return (sigma_first, sigma_second)


def solution(mesh):
    return jax.shard_map(
        body,
        mesh=mesh,
        in_specs=(
            P("blk", "col", None),
            P("blk"),
            P("blk", None),
            P("blk", "col", None, None),
            P("col", None, None),
        ),
        out_specs=(P("blk", "col", None), P("blk", "col", None)),
        check_vma=False,
    )
```

profile of v0, /device:TPU:7, one launch (start us, length us, event | category | flops | bytes accessed | tf_op | source)
XLA Modules:
  0.0 155.4 jit_solution(1749032536322166111)
XLA Ops:
  7.3 0.8 iota_compare_fusion
  8.1 0.7 broadcast_compare_fusion
  8.8 1.1 and_select_fusion.2
  10.0 2.5 %all_gather.6 = bf16[2,384,384]{2,1,0:T(8,128)(2,1)S(1)} all-gather(bf16[2,192,384]{2,1,0:T(8,128)(2,1)S(1)} %and_select_fusion.2), channel_id=1, replica_groups=mesh['blk'=16,'col'=2] {'col'}, dimensions={1}, use_global_device_ids=true | all-gather | bytes 884736 | tf_op jit(solution)/shard_map/all_gather | solution.py:34
  12.5 2.2 %collective-permute-start.1 = (bf16[2,384,384]{2,1,0:T(8,128)(2,1)S(1)}, bf16[2,384,384]{2,1,0:T(8,128)(2,1)S(1)}, u32[]{:S(2)}, u32[]{:S(2)}) collective-permute-start(bf16[2,384,384]{2,1,0:T(8,128)(2,1)S(1)} %all_gather.6), channel_id=1, source_target_pairs={{2,0},{4,2},{6,4},{8,6},{10,8},{12,10},{14,12},{16,14},{18,16},{20... | collective-permute-start | bytes 1769480 | tf_op jit(solution)/shard_map/ppermute | solution.py:17
  14.6 4.9 %collective-permute-start = (bf16[2,384,384]{2,1,0:T(8,128)(2,1)S(1)}, bf16[2,384,384]{2,1,0:T(8,128)(2,1)S(1)}, u32[]{:S(2)}, u32[]{:S(2)}) collective-permute-start(bf16[2,384,384]{2,1,0:T(8,128)(2,1)S(1)} %all_gather.6), channel_id=1, source_target_pairs={{0,2},{2,4},{4,6},{6,8},{8,10},{10,12},{12,14},{14,16},{16,18},{18... | collective-permute-start | bytes 1769480 | tf_op jit(solution)/shard_map/ppermute | solution.py:14
  19.6 0.2 slice_reduce_fusion.4
  19.8 10.9 %collective-permute-done.1 = bf16[2,384,384]{2,1,0:T(8,128)(2,1)S(1)} collective-permute-done((bf16[2,384,384]{2,1,0:T(8,128)(2,1)S(1)}, bf16[2,384,384]{2,1,0:T(8,128)(2,1)S(1)}, u32[]{:S(2)}, u32[]{:S(2)}) %collective-permute-start.1) | collective-permute-done | bytes 589856 | tf_op jit(solution)/shard_map/ppermute | solution.py:17
  30.8 10.7 %collective-permute-done = bf16[2,384,384]{2,1,0:T(8,128)(2,1)S(1)} collective-permute-done((bf16[2,384,384]{2,1,0:T(8,128)(2,1)S(1)}, bf16[2,384,384]{2,1,0:T(8,128)(2,1)S(1)}, u32[]{:S(2)}, u32[]{:S(2)}) %collective-permute-start) | collective-permute-done | bytes 589856 | tf_op jit(solution)/shard_map/ppermute | solution.py:14
  41.5 0.8 copy-done.5
  42.3 3.9 %fusion.2 = bf16[2,384,384]{2,1,0:T(8,128)(2,1)} fusion(bf16[2,2,384,384]{3,2,1,0:T(8,128)(2,1)S(1)} %copy-done, bf16[2,384,384]{2,1,0:T(8,128)(2,1)S(1)} %copy-done.4, bf16[2,384,384]{2,1,0:T(8,128)(2,1)S(1)} %collective-permute-done.1, bf16[2,384,384]{2,1,0:T(8,128)(2,1)S(1)} %all_gather.6, bf16[2,384,384]{2,1,0:T(8,128)(2,1)} %copy-done.5, ...), kind=kOutput, calls=%fused_computation.6 | convolution fusion | flops 913047552 | bytes 4128808 | tf_op jit(solution)/shard_map/swac,wdc->sad/dot_general | solution.py:40
  46.3 10.6 %reduce-scatter.3.cloned.1.call-done = bf16[2,192,384]{2,1,0:T(8,128)(2,1)} async-done(((bf16[2,384,384]{2,1,0:T(8,128)(2,1)}), bf16[2,192,384]{2,1,0:T(8,128)(2,1)}) %reduce-scatter.3.cloned.1.call-update) | async-done | bytes 294928 | tf_op jit(solution)/shard_map/reduce_scatter | solution.py:41
  56.9 1.9 %fusion.5 = (f32[]{:T(128)}, f32[]{:T(128)}, f32[2,192,384]{2,1,0:T(8,128)S(1)}) fusion(bf16[2,192,384]{2,1,0:T(8,128)(2,1)} %reduce-scatter.3.cloned.1.call-done, pred[2,384]{1,0:T(4,128)(4,1)S(1)} %iota_compare_fusion, pred[2,192]{1,0:T(4,128)(4,1)S(1)} %broadcast_compare_fusion, bf16[2,192,384]{2,1,0:T(8,128)(2,1)S(1)} %copy-done.1), kind=kLoop, calls=%fused_computation.17 | loop fusion | flops 1474558 | bytes 1180808 | tf_op jit(solution)/shard_map/reduce_sum | solution.py:60
  58.8 39.4 %all-reduce = (f32[]{:T(128)}, f32[]{:T(128)}) all-reduce(f32[]{:T(128)} %get-tuple-element.3, f32[]{:T(128)} %get-tuple-element.2), channel_id=1, replica_groups=mesh['blk'=16,'col'=2] {'blk','col'}, use_global_device_ids=true, to_apply=%region_2.3 | all-reduce | flops 2 | bytes 16 | tf_op jit(solution)/shard_map/psum | solution.py:59
  99.6 0.2 fusion.7
  99.8 3.3 %all_gather.7 = bf16[2,384,384]{2,1,0:T(8,128)(2,1)S(1)} all-gather(bf16[2,192,384]{2,1,0:T(8,128)(2,1)S(1)} %fusion.7), channel_id=1, replica_groups=mesh['blk'=16,'col'=2] {'col'}, dimensions={1}, use_global_device_ids=true | all-gather | bytes 884736 | tf_op jit(solution)/shard_map/all_gather | solution.py:34
  103.1 3.1 %collective-permute-start.3 = (bf16[2,384,384]{2,1,0:T(8,128)(2,1)S(1)}, bf16[2,384,384]{2,1,0:T(8,128)(2,1)S(1)}, u32[]{:S(2)}, u32[]{:S(2)}) collective-permute-start(bf16[2,384,384]{2,1,0:T(8,128)(2,1)S(1)} %all_gather.7), channel_id=1, source_target_pairs={{2,0},{4,2},{6,4},{8,6},{10,8},{12,10},{14,12},{16,14},{18,16},{20... | collective-permute-start | bytes 1769480 | tf_op jit(solution)/shard_map/ppermute | solution.py:17
  106.2 4.0 %collective-permute-start.2 = (bf16[2,384,384]{2,1,0:T(8,128)(2,1)S(1)}, bf16[2,384,384]{2,1,0:T(8,128)(2,1)}, u32[]{:S(2)}, u32[]{:S(2)}) collective-permute-start(bf16[2,384,384]{2,1,0:T(8,128)(2,1)S(1)} %all_gather.7), channel_id=1, source_target_pairs={{0,2},{2,4},{4,6},{6,8},{8,10},{10,12},{12,14},{14,16},{16,18},{18... | collective-permute-start | bytes 1769480 | tf_op jit(solution)/shard_map/ppermute | solution.py:14
  110.2 11.2 %collective-permute-done.3 = bf16[2,384,384]{2,1,0:T(8,128)(2,1)S(1)} collective-permute-done((bf16[2,384,384]{2,1,0:T(8,128)(2,1)S(1)}, bf16[2,384,384]{2,1,0:T(8,128)(2,1)S(1)}, u32[]{:S(2)}, u32[]{:S(2)}) %collective-permute-start.3) | collective-permute-done | bytes 589856 | tf_op jit(solution)/shard_map/ppermute | solution.py:17
  121.4 0.8 copy-done.6
  122.2 10.7 %collective-permute-done.2 = bf16[2,384,384]{2,1,0:T(8,128)(2,1)} collective-permute-done((bf16[2,384,384]{2,1,0:T(8,128)(2,1)S(1)}, bf16[2,384,384]{2,1,0:T(8,128)(2,1)}, u32[]{:S(2)}, u32[]{:S(2)}) %collective-permute-start.2) | collective-permute-done | bytes 589856 | tf_op jit(solution)/shard_map/ppermute | solution.py:14
  132.9 4.2 %fusion.3 = bf16[2,384,384]{2,1,0:T(8,128)(2,1)} fusion(bf16[2,2,384,384]{3,2,1,0:T(8,128)(2,1)S(1)} %copy-done, bf16[2,384,384]{2,1,0:T(8,128)(2,1)S(1)} %copy-done.4, bf16[2,384,384]{2,1,0:T(8,128)(2,1)} %copy-done.6, bf16[2,384,384]{2,1,0:T(8,128)(2,1)S(1)} %all_gather.7, bf16[2,384,384]{2,1,0:T(8,128)(2,1)} %collective-permute-done.2, ...), kind=kOutput, calls=%fused_computation.7 | convolution fusion | flops 913047552 | bytes 4128808 | tf_op jit(solution)/shard_map/swac,wdc->sad/dot_general | solution.py:40
  137.2 9.5 %reduce-scatter.5.cloned.1.call-done = bf16[2,192,384]{2,1,0:T(8,128)(2,1)} async-done(((bf16[2,384,384]{2,1,0:T(8,128)(2,1)}), bf16[2,192,384]{2,1,0:T(8,128)(2,1)}) %reduce-scatter.5.cloned.1.call-update) | async-done | bytes 294928 | tf_op jit(solution)/shard_map/reduce_scatter | solution.py:41
  146.7 1.9 %and_select_fusion = f32[2,192,384]{2,1,0:T(8,128)} fusion(bf16[2,192,384]{2,1,0:T(8,128)(2,1)} %reduce-scatter.5.cloned.1.call-done, pred[2,384]{1,0:T(4,128)(4,1)S(1)} %iota_compare_fusion, pred[2,192]{1,0:T(4,128)(4,1)S(1)} %broadcast_compare_fusion), kind=kLoop, calls=%fused_computation.10 | loop fusion | flops 589824 | bytes 885888 | tf_op jit(solution)/shard_map/jit(_where)/select_n | solution.py:44
  (18 shorter events, 0.1 us)
Async XLA Ops:
  7.2 35.1 %copy-start = (bf16[2,2,384,384]{3,2,1,0:T(8,128)(2,1)S(1)}, bf16[2,2,384,384]{3,2,1,0:T(8,128)(2,1)}, u32[]{:S(2)}) copy-start(bf16[2,2,384,384]{3,2,1,0:T(8,128)(2,1)} %param.8) | copy-start | bytes 3538948
  7.2 12.4 %copy-start.3 = (s32[2,5]{1,0:T(2,128)S(1)}, s32[2,5]{1,0:T(2,128)}, u32[]{:S(2)}) copy-start(s32[2,5]{1,0:T(2,128)} %param.7) | copy-start | bytes 124
  7.2 35.1 %copy-start.4 = (bf16[2,384,384]{2,1,0:T(8,128)(2,1)S(1)}, bf16[2,384,384]{2,1,0:T(8,128)(2,1)}, u32[]{:S(2)}) copy-start(bf16[2,384,384]{2,1,0:T(8,128)(2,1)} %param.9) | copy-start | bytes 1769476
  7.2 49.7 %reduce-scatter.3.cloned.1.call-start = ((), (), s32[]{:S(2)}) async-start(), calls=%async_computation.2 | async-start | bytes 884736 | tf_op jit(solution)/shard_map/reduce_scatter | solution.py:41
  12.5 18.3 %collective-permute-start.1 = (bf16[2,384,384]{2,1,0:T(8,128)(2,1)S(1)}, bf16[2,384,384]{2,1,0:T(8,128)(2,1)S(1)}, u32[]{:S(2)}, u32[]{:S(2)}) collective-permute-start(bf16[2,384,384]{2,1,0:T(8,128)(2,1)S(1)} %all_gather.6), channel_id=1, source_target_pairs={{2,0},{4,2},{6,4},{8,6},{10,8},{12,10},{14,12},{16,14},{18,16},{20... | collective-permute-start | bytes 1769480 | tf_op jit(solution)/shard_map/ppermute | solution.py:17
  14.6 26.8 %collective-permute-start = (bf16[2,384,384]{2,1,0:T(8,128)(2,1)S(1)}, bf16[2,384,384]{2,1,0:T(8,128)(2,1)S(1)}, u32[]{:S(2)}, u32[]{:S(2)}) collective-permute-start(bf16[2,384,384]{2,1,0:T(8,128)(2,1)S(1)} %all_gather.6), channel_id=1, source_target_pairs={{0,2},{2,4},{4,6},{6,8},{8,10},{10,12},{12,14},{14,16},{16,18},{18... | collective-permute-start | bytes 1769480 | tf_op jit(solution)/shard_map/ppermute | solution.py:14
  41.5 0.8 copy-start.5
  42.3 14.6 %copy-start.1 = (bf16[2,192,384]{2,1,0:T(8,128)(2,1)S(1)}, bf16[2,192,384]{2,1,0:T(8,128)(2,1)}, u32[]{:S(2)}) copy-start(bf16[2,192,384]{2,1,0:T(8,128)(2,1)} %param.5) | copy-start | bytes 884740
  46.3 100.4 %reduce-scatter.5.cloned.1.call-start = ((), (), s32[]{:S(2)}) async-start(), calls=%async_computation.3 | async-start | bytes 884736 | tf_op jit(solution)/shard_map/reduce_scatter | solution.py:41
  58.8 78.3 %copy-start.2 = (f32[2,192,384]{2,1,0:T(8,128)}, f32[2,192,384]{2,1,0:T(8,128)S(1)}, u32[]{:S(2)}) copy-start(f32[2,192,384]{2,1,0:T(8,128)S(1)} %get-tuple-element.11) | copy-start | bytes 1769476
  103.1 18.3 %collective-permute-start.3 = (bf16[2,384,384]{2,1,0:T(8,128)(2,1)S(1)}, bf16[2,384,384]{2,1,0:T(8,128)(2,1)S(1)}, u32[]{:S(2)}, u32[]{:S(2)}) collective-permute-start(bf16[2,384,384]{2,1,0:T(8,128)(2,1)S(1)} %all_gather.7), channel_id=1, source_target_pairs={{2,0},{4,2},{6,4},{8,6},{10,8},{12,10},{14,12},{16,14},{18,16},{20... | collective-permute-start | bytes 1769480 | tf_op jit(solution)/shard_map/ppermute | solution.py:17
  106.2 26.7 %collective-permute-start.2 = (bf16[2,384,384]{2,1,0:T(8,128)(2,1)S(1)}, bf16[2,384,384]{2,1,0:T(8,128)(2,1)}, u32[]{:S(2)}, u32[]{:S(2)}) collective-permute-start(bf16[2,384,384]{2,1,0:T(8,128)(2,1)S(1)} %all_gather.7), channel_id=1, source_target_pairs={{0,2},{2,4},{4,6},{6,8},{8,10},{10,12},{12,14},{14,16},{16,18},{18... | collective-permute-start | bytes 1769480 | tf_op jit(solution)/shard_map/ppermute | solution.py:14
  121.4 0.8 copy-start.6
Sparse Core Ops, SparseCore 0:
  46.4 10.4 reduce-scatter.2
  137.3 9.3 reduce-scatter.4
where the time goes:
time: 157 us; the launch traced here: 155 us
  waiting for transfers between devices  63.7 us (41%)
  blocking collectives  45.2 us (29%)
  between operations  15.5 us (10%)
  starting transfers between devices  14.2 us (9%)
  matrix products  8.14 us (5%)
  other arithmetic  6.71 us (4%)
  local copies, waits for them, and re-layouts  1.87 us (1%)
    psum x1, blocking collectives, body(): lax.psum((jnp.sum(psi_float * sigma_first), jnp.sum(psi_float * psi_float...  39.4 us
    ppermute x2, waiting for transfers between devices, with_halo(): lax.ppermute(lax.slice_in_dim(block, 0, width, axis=dim), axis, backward)  22.1 us
    ppermute x2, waiting for transfers between devices, with_halo(): lax.ppermute(lax.slice_in_dim(block, block.shape[dim] - width, None, axis...  21.5 us
    reduce_scatter x2, waiting for transfers between devices, apply_hamiltonian(): lax.psum_scatter(partial_term.astype(jnp.bfloat16), 'col', scatter_dimens...  20.1 us
    ppermute x2, starting transfers between devices, with_halo(): lax.ppermute(lax.slice_in_dim(block, block.shape[dim] - width, None, axis...  8.89 us
    dot_general x2, matrix products, apply_hamiltonian(): jnp.einsum('swac,wdc->sad', temp, right_env, preferred_element_type=jnp.f...  8.14 us
    all_gather x2, blocking collectives, apply_hamiltonian(): full = lax.all_gather(vector, 'col', axis=1, tiled=True)  5.85 us
    ppermute x2, starting transfers between devices, with_halo(): lax.ppermute(lax.slice_in_dim(block, 0, width, axis=dim), axis, backward)  5.25 us
  transfers between devices with their start and end apart: 6, of which 6 were waited for; matrix products, arithmetic and copies ran while one was open for 0% of the time, Pallas kernels for 0%

commit v1 on v0

v1 whole, which is shorter than its diff:
```python
import functools

import jax
import jax.numpy as jnp
from jax import lax
from jax.experimental import pallas as pl
from jax.experimental.pallas import tpu as pltpu
from jax.sharding import PartitionSpec as P

MESH = pl.DeviceIdType.MESH
LANES = 128
HALVES = 2


def kernel(
    n_blk,
    n_col,
    dims,
    pattern,
    psi,
    left_env,
    right_env,
    first_out,
    second_out,
    raw,
    own,
    near,
    far,
    z,
    z_psi,
    left,
    right,
    acc,
    sig,
    stat_own,
    stat_col,
    stat_sum,
    stat_blk,
    local_sem,
    near_send,
    near_recv,
    far_send,
    far_recv,
    z_send,
    z_recv,
    env_send,
    env_recv,
    stat_col_send,
    stat_col_recv,
    stat_blk_send,
    stat_blk_recv,
):
    b = lax.axis_index("blk")
    c = lax.axis_index("col")
    sectors, rows, width = psi.shape
    terms = left_env.shape[1]
    all_terms = terms * n_col
    pieces = width // LANES
    height = rows // HALVES
    chunks = [(p, r) for p in range(pieces) for r in range(HALVES)]
    even = lax.rem(b, 2) == 0
    pair = b + 1 - 2 * lax.rem(b, 2)
    onward = b + 2 - 4 * lax.rem(b, 2)
    source = b - 2 + 4 * lax.rem(b, 2)
    has_onward = (onward >= 0) & (onward < n_blk)
    has_source = (source >= 0) & (source < n_blk)
    my_rows = pl.ds(pl.multiple_of(c * rows, 16), rows)

    load_psi = pltpu.make_async_copy(psi, raw, local_sem.at[0])
    load_psi.start()
    load_left = pltpu.make_async_copy(
        left_env.at[:, :, my_rows, :], left.at[:, pl.ds(c * terms, terms)], local_sem.at[1]
    )
    load_left.start()
    load_right = pltpu.make_async_copy(
        right_env, right.at[pl.ds(c * terms, terms)], local_sem.at[2]
    )
    load_right.start()

    barrier = pltpu.get_barrier_semaphore()

    @pl.loop(1, n_blk)
    def _(i):
        pl.semaphore_signal(
            barrier, inc=1, device_id=(lax.rem(b + i, n_blk), c), device_id_type=MESH
        )

    for k in range(1, n_col):
        pl.semaphore_signal(
            barrier, inc=1, device_id=(b, lax.rem(c + k, n_col)), device_id_type=MESH
        )

    load_psi.wait()
    row_ids = c * rows + lax.broadcasted_iota(jnp.int32, (rows, width), 0)
    col_ids = lax.broadcasted_iota(jnp.int32, (rows, width), 1)
    furthest = jnp.maximum(row_ids, col_ids)
    for s in range(sectors):
        own[0, s] = jnp.where(
            furthest < dims[s], raw[s].astype(jnp.float32), 0.0
        ).astype(jnp.bfloat16)

    @pl.when(jnp.logical_not(has_source))
    def _():
        far[...] = jnp.zeros_like(far)

    pl.semaphore_wait(barrier, n_blk + n_col - 2)

    def cut(ref, h, i):
        p, r = chunks[i]
        return ref.at[h, :, pl.ds(r * height, height), pl.ds(p * LANES, LANES)]

    def to_pair(h, i):
        return pltpu.make_async_remote_copy(
            src_ref=cut(own, h, i),
            dst_ref=cut(near, h, i),
            send_sem=near_send.at[h, i],
            recv_sem=near_recv.at[h, i],
            device_id=(pair, c),
            device_id_type=MESH,
        )

    def to_onward(h, i):
        return pltpu.make_async_remote_copy(
            src_ref=cut(near, h, i),
            dst_ref=cut(far, h, i),
            send_sem=far_send.at[h, i],
            recv_sem=far_recv.at[h, i],
            device_id=(onward, c),
            device_id_type=MESH,
        )

    def z_part(h, i, holder):
        p, r = chunks[i]
        start = pl.multiple_of(holder * rows + r * height, 16)
        return z.at[h, :, pl.ds(start, height), pl.ds(p * LANES, LANES)]

    def z_copy(h, i, k, holder):
        return pltpu.make_async_remote_copy(
            src_ref=z_part(h, i, holder),
            dst_ref=z_part(h, i, holder),
            send_sem=z_send.at[h, k - 1, i],
            recv_sem=z_recv.at[h, k - 1, i],
            device_id=(b, lax.rem(c + k, n_col)),
            device_id_type=MESH,
        )

    def env_copies(k, holder, taker):
        took = pl.ds(pl.multiple_of(taker * rows, 16), rows)
        slot = pl.ds(holder * terms, terms)
        return [
            pltpu.make_async_remote_copy(
                src_ref=src,
                dst_ref=dst,
                send_sem=env_send.at[k - 1, j],
                recv_sem=env_recv.at[k - 1, j],
                device_id=(b, lax.rem(c + k, n_col)),
                device_id_type=MESH,
            )
            for j, (src, dst) in enumerate(
                [
                    (left_env.at[:, :, took, :], left.at[:, slot]),
                    (right_env, right.at[slot]),
                ]
            )
        ]

    def start_halo(h):
        for i in range(len(chunks)):
            to_pair(h, i).start()

    start_halo(0)
    for k in range(1, n_col):
        for copy in env_copies(k, c, lax.rem(c + k, n_col)):
            copy.start()

    coeff = [[pattern[s, j].astype(jnp.float32) for j in range(5)] for s in range(2)]
    zero = jnp.float32(0.0)
    below = ((coeff[0][0], coeff[0][1]), (zero, coeff[1][0]))
    above = ((coeff[0][4], zero), (coeff[1][3], coeff[1][4]))
    inner = ((coeff[0][2], coeff[0][3]), (coeff[1][1], coeff[1][2]))
    near_c = [[jnp.where(even, above[s][k], below[s][k]) for k in range(2)] for s in range(2)]
    far_c = [[jnp.where(even, below[s][k], above[s][k]) for k in range(2)] for s in range(2)]

    def combine(h, i, theta):
        p, r = chunks[i]
        rr, cc = slice(r * height, (r + 1) * height), slice(p * LANES, (p + 1) * LANES)
        start = pl.multiple_of(c * rows + r * height, 16)
        total = [None, None]
        for ref, weights in ((own, inner), (near, near_c), (far, far_c)):
            for k in range(2):
                block = ref[h, k, rr, cc].astype(jnp.float32)
                for s in range(2):
                    term = weights[s][k] * block
                    total[s] = term if total[s] is None else total[s] + term
        for s in range(2):
            if h == 0:
                z_psi[s, rr, cc] = total[s]
            else:
                total[s] = total[s] - theta * z_psi[s, rr, cc]
            z[h, s, pl.ds(start, height), cc] = total[s].astype(jnp.bfloat16)

    def product(h, p):
        cc = slice(p * LANES, (p + 1) * LANES)
        temp = []
        for s in range(2):
            t = jnp.dot(
                left[s].reshape(all_terms * rows, width),
                z[h, s, :, cc],
                preferred_element_type=jnp.float32,
            ).astype(jnp.bfloat16)
            temp.append(t)
        wide = jnp.concatenate(
            [
                jnp.concatenate([t[w * rows : (w + 1) * rows] for t in temp], axis=0)
                for w in range(all_terms)
            ],
            axis=1,
        )
        weights = jnp.concatenate([right[w, :, cc] for w in range(all_terms)], axis=1)
        part = lax.dot_general(
            wide, weights, (((1,), (1,)), ((), ())), preferred_element_type=jnp.float32
        )
        if p == 0:
            acc[...] = part
        else:
            acc[...] += part

    def finish_piece(h, p):
        for r in range(HALVES):
            for k in range(1, n_col):
                z_copy(h, p * HALVES + r, k, lax.rem(c + n_col - k, n_col)).wait_recv()
        if h == 0 and p == 0:
            load_left.wait()
            load_right.wait()
            for k in range(1, n_col):
                for copy in env_copies(k, lax.rem(c + n_col - k, n_col), c):
                    copy.wait_recv()
        product(h, p)

    def apply(h, theta_of):
        theta = None
        count = len(chunks)
        for i in range(count + 2):
            if i < count:
                to_pair(h, i).wait_recv()

                @pl.when(has_onward)
                def _():
                    to_onward(h, i).start()

            j = i - 1
            if 0 <= j < count:

                @pl.when(has_source)
                def _():
                    to_onward(h, j).wait_recv()

                if j == 0 and theta_of is not None:
                    theta = theta_of()
                combine(h, j, theta)
                for k in range(1, n_col):
                    z_copy(h, j, k, c).start()
            j = i - 2
            if j >= 0 and j % HALVES == HALVES - 1:
                finish_piece(h, j // HALVES)

    def masked(s):
        return jnp.where(
            furthest < dims[s],
            acc[s * rows : (s + 1) * rows, :] * (1.0 / float(all_terms) ** 0.5),
            0.0,
        )

    def fold(x):
        x = jnp.sum(x.reshape(rows // 8, 8, width), axis=0)
        out = x[:, :LANES]
        for p in range(1, pieces):
            out = out + x[:, p * LANES : (p + 1) * LANES]
        return out

    apply(0, None)
    for s in range(2):
        sig[0, s] = masked(s)
        own[1, s] = sig[0, s].astype(jnp.bfloat16)
    start_halo(1)
    for q in range(2):
        total = None
        for s in range(2):
            v = own[0, s].astype(jnp.float32)
            term = fold(v * (sig[0, s] if q == 0 else v))
            total = term if total is None else total + term
        stat_own[q] = total

    def stat_to_col(k):
        return pltpu.make_async_remote_copy(
            src_ref=stat_own,
            dst_ref=stat_col.at[k - 1],
            send_sem=stat_col_send.at[k - 1],
            recv_sem=stat_col_recv.at[k - 1],
            device_id=(b, lax.rem(c + k, n_col)),
            device_id_type=MESH,
        )

    def stat_to_blk(i):
        return pltpu.make_async_remote_copy(
            src_ref=stat_sum,
            dst_ref=stat_blk.at[i - 1],
            send_sem=stat_blk_send.at[i - 1],
            recv_sem=stat_blk_recv.at[i - 1],
            device_id=(lax.rem(b + i, n_blk), c),
            device_id_type=MESH,
        )

    for k in range(1, n_col):
        stat_to_col(k).start()
    store_first = pltpu.make_async_copy(sig.at[0], first_out, local_sem.at[3])
    store_first.start()
    for k in range(1, n_col):
        stat_to_col(k).wait_recv()
    total = stat_own[...]
    for k in range(1, n_col):
        total = total + stat_col[k - 1]
    stat_sum[...] = total

    @pl.loop(1, n_blk)
    def _(i):
        stat_to_blk(i).start()

    def theta_of():
        @pl.loop(1, n_blk)
        def _(i):
            stat_to_blk(i).wait_recv()

        total = stat_sum[...] + jnp.sum(stat_blk[...], axis=0)
        sums = [jnp.sum(total[q], axis=(0, 1), keepdims=True) for q in range(2)]
        return sums[0] / sums[1]

    apply(1, theta_of)
    for s in range(2):
        sig[1, s] = masked(s)
    store_second = pltpu.make_async_copy(sig.at[1], second_out, local_sem.at[4])
    store_second.start()

    for h in range(2):
        for i in range(len(chunks)):
            to_pair(h, i).wait_send()
            for k in range(1, n_col):
                z_copy(h, i, k, c).wait_send()

        @pl.when(has_onward)
        def _():
            for i in range(len(chunks)):
                to_onward(h, i).wait_send()

    for k in range(1, n_col):
        for copy in env_copies(k, c, lax.rem(c + k, n_col)):
            copy.wait_send()
        stat_to_col(k).wait_send()

    @pl.loop(1, n_blk)
    def _(i):
        stat_to_blk(i).wait_send()

    store_first.wait()
    store_second.wait()


def body(n_blk, n_col, psi, dims, pattern, left_env, right_env):
    sectors, rows, width = psi.shape
    terms = left_env.shape[1] * n_col
    chunks = (width // LANES) * HALVES
    bf16, f32 = jnp.bfloat16, jnp.float32
    dma = pltpu.SemaphoreType.DMA
    vmem = pltpu.VMEM
    hbm = pl.BlockSpec(memory_space=pl.ANY)
    smem = pl.BlockSpec(memory_space=pltpu.SMEM)
    out = jax.ShapeDtypeStruct(psi.shape, f32)
    return pl.pallas_call(
        functools.partial(kernel, n_blk, n_col),
        out_shape=(out, out),
        in_specs=[smem, smem, hbm, hbm, hbm],
        out_specs=(hbm, hbm),
        scratch_shapes=[
            vmem((sectors, rows, width), bf16),
            vmem((2, sectors, rows, width), bf16),
            vmem((2, sectors, rows, width), bf16),
            vmem((2, sectors, rows, width), bf16),
            vmem((2, sectors, width, width), bf16),
            vmem((sectors, rows, width), f32),
            vmem((sectors, terms, rows, width), bf16),
            vmem((terms, width, width), bf16),
            vmem((sectors * rows, width), f32),
            vmem((2, sectors, rows, width), f32),
            vmem((2, 8, LANES), f32),
            vmem((n_col - 1, 2, 8, LANES), f32),
            vmem((2, 8, LANES), f32),
            vmem((n_blk - 1, 2, 8, LANES), f32),
            dma((5,)),
            dma((2, chunks)),
            dma((2, chunks)),
            dma((2, chunks)),
            dma((2, chunks)),
            dma((2, n_col - 1, chunks)),
            dma((2, n_col - 1, chunks)),
            dma((n_col - 1, 2)),
            dma((n_col - 1, 2)),
            dma((n_col - 1,)),
            dma((n_col - 1,)),
            dma((n_blk - 1,)),
            dma((n_blk - 1,)),
        ],
        compiler_params=pltpu.CompilerParams(
            collective_id=0, has_side_effects=True, vmem_limit_bytes=40 * 1024 * 1024
        ),
    )(dims, pattern, psi, left_env, right_env)


def solution(mesh):
    return jax.shard_map(
        functools.partial(body, mesh.shape["blk"], mesh.shape["col"]),
        mesh=mesh,
        in_specs=(
            P("blk", "col", None),
            P("blk"),
            P("blk", None),
            P("blk", "col", None, None),
            P("col", None, None),
        ),
        out_specs=(P("blk", "col", None), P("blk", "col", None)),
        check_vma=False,
    )
```

time: 157 us -> 50.1 us (0.32)
  waiting for transfers between devices: 63.7 us -> 0 us
  blocking collectives: 45.2 us -> 0 us
  Pallas kernels: 0 us -> 42.2 us
  between operations: 15.5 us -> 0.65 us
  starting transfers between devices: 14.2 us -> 0 us
  matrix products: 8.14 us -> 0 us
  other arithmetic: 6.71 us -> 0 us
  local copies, waits for them, and re-layouts: 1.87 us -> 6.25 us
    ppermute x4 -> x0, waiting for transfers between devices: 43.6 us -> none  [the longest x2 22.1 us: with_halo(): lax.ppermute(lax.slice_in_dim(block, 0, width, axis=dim), axis, backward)]
    pallas_call x0 -> x1, Pallas kernels: none -> 42.2 us  [body(): pl.pallas_call(functools.partial(kernel, n_blk, n_col), out_shape=(out, o...]
    psum x1 -> x0, blocking collectives: 39.4 us -> none  [body(): lax.psum((jnp.sum(psi_float * sigma_first), jnp.sum(psi_float * psi_float...]
    reduce_scatter x2 -> x0, waiting for transfers between devices: 20.1 us -> none  [apply_hamiltonian(): lax.psum_scatter(partial_term.astype(jnp.bfloat16), 'col', scatter_dimens...]
    ppermute x4 -> x0, starting transfers between devices: 14.1 us -> none  [the longest x2 8.89 us: with_halo(): lax.ppermute(lax.slice_in_dim(block, block.shape[dim] - width, None, axis...]
    dot_general x2 -> x0, matrix products: 8.14 us -> none  [apply_hamiltonian(): jnp.einsum('swac,wdc->sad', temp, right_env, preferred_element_type=jnp.f...]
    all_gather x2 -> x0, blocking collectives: 5.85 us -> none  [apply_hamiltonian(): full = lax.all_gather(vector, 'col', axis=1, tiled=True)]
    unnamed x14 -> x12, local copies, waits for them, and re-layouts: 1.65 us -> 6.25 us
  transfers between devices with their start and end apart: 6 -> 0, of which waited for: 6 -> 0; matrix products, arithmetic and copies ran while one was open for 0% -> 0% of each run, Pallas kernels for 0% -> 0%
where the time goes in v1:
time: 50.1 us; the launch traced here: 49.1 us
  Pallas kernels  42.2 us (84%)
  local copies, waits for them, and re-layouts  6.25 us (12%)
  between operations  0.65 us (1%)
    pallas_call x1, Pallas kernels, body(): pl.pallas_call(functools.partial(kernel, n_blk, n_col), out_shape=(out, o...  42.2 us
    unnamed x12, local copies, waits for them, and re-layouts  6.25 us

profile of v1, /device:TPU:7, one launch (start us, length us, event | category | flops | bytes accessed | tf_op | source)
XLA Modules:
  0.0 49.1 jit_solution(10978690859215573687)
XLA Ops:
  0.6 0.0 copy-start
  0.6 1.3 %copy-done = bf16[2,2,384,384]{3,2,1,0:T(8,128)(2,1)S(1)} copy-done((bf16[2,2,384,384]{3,2,1,0:T(8,128)(2,1)S(1)}, bf16[2,2,384,384]{3,2,1,0:T(8,128)(2,1)}, u32[]{:S(2)}) %copy-start) | copy-done | bytes 1179672
  1.9 0.0 copy-start.1
  1.9 1.1 %copy-done.1 = bf16[2,384,384]{2,1,0:T(8,128)(2,1)S(1)} copy-done((bf16[2,384,384]{2,1,0:T(8,128)(2,1)S(1)}, bf16[2,384,384]{2,1,0:T(8,128)(2,1)}, u32[]{:S(2)}) %copy-start.1) | copy-done | bytes 589848
  3.0 0.0 copy-start.2
  3.0 1.0 %copy-done.2 = bf16[2,192,384]{2,1,0:T(8,128)(2,1)S(1)} copy-done((bf16[2,192,384]{2,1,0:T(8,128)(2,1)S(1)}, bf16[2,192,384]{2,1,0:T(8,128)(2,1)}, u32[]{:S(2)}) %copy-start.2) | copy-done | bytes 294936
  3.9 0.0 copy-start.3
  3.9 0.7 %copy-done.3 = s32[2,5]{1,0:T(2,128)S(1)} copy-done((s32[2,5]{1,0:T(2,128)S(1)}, s32[2,5]{1,0:T(2,128)}, u32[]{:S(2)}) %copy-start.3) | copy-done | bytes 64
  4.6 0.0 copy-start.4
  4.6 0.7 %copy-done.4 = s32[2]{0:T(128)S(1)} copy-done((s32[2]{0:T(128)S(1)}, s32[2]{0:T(128)}, u32[]{:S(2)}) %copy-start.4) | copy-done | bytes 32
  5.3 42.2 %shard_map.68 = (f32[2,192,384]{2,1,0:T(8,128)S(1)}, f32[2,192,384]{2,1,0:T(8,128)S(1)}) custom-call(s32[2]{0:T(128)S(1)} %copy-done.4, s32[2,5]{1,0:T(2,128)S(1)} %copy-done.3, bf16[2,192,384]{2,1,0:T(8,128)(2,1)S(1)} %copy-done.2, bf16[2,2,384,384]{3,2,1,0:T(8,128)(2,1)S(1)} %copy-done, bf16[2,384,384]{2,1,0:T(8,128)(2,1)S(1)} %copy-done.1), custom_call_target="tpu_custom_call" | custom-call | tf_op jit(solution)/shard_map/pallas_call | solution.py:378
  47.5 0.8 %copy.9 = f32[2,192,384]{2,1,0:T(8,128)} copy(f32[2,192,384]{2,1,0:T(8,128)S(1)} %get-tuple-element.4) | data formatting | bytes 1179648
  48.3 0.8 %copy.10 = f32[2,192,384]{2,1,0:T(8,128)} copy(f32[2,192,384]{2,1,0:T(8,128)S(1)} %get-tuple-element.5) | data formatting | bytes 1179648
Async XLA Ops:
  0.6 1.3 %copy-start = (bf16[2,2,384,384]{3,2,1,0:T(8,128)(2,1)S(1)}, bf16[2,2,384,384]{3,2,1,0:T(8,128)(2,1)}, u32[]{:S(2)}) copy-start(bf16[2,2,384,384]{3,2,1,0:T(8,128)(2,1)} %left_env.1) | copy-start | bytes 3538948
  1.9 1.1 %copy-start.1 = (bf16[2,384,384]{2,1,0:T(8,128)(2,1)S(1)}, bf16[2,384,384]{2,1,0:T(8,128)(2,1)}, u32[]{:S(2)}) copy-start(bf16[2,384,384]{2,1,0:T(8,128)(2,1)} %right_env.1) | copy-start | bytes 1769476
  3.0 1.0 %copy-start.2 = (bf16[2,192,384]{2,1,0:T(8,128)(2,1)S(1)}, bf16[2,192,384]{2,1,0:T(8,128)(2,1)}, u32[]{:S(2)}) copy-start(bf16[2,192,384]{2,1,0:T(8,128)(2,1)} %psi.1) | copy-start | bytes 884740
  3.9 0.7 %copy-start.3 = (s32[2,5]{1,0:T(2,128)S(1)}, s32[2,5]{1,0:T(2,128)}, u32[]{:S(2)}) copy-start(s32[2,5]{1,0:T(2,128)} %pattern.1) | copy-start | bytes 124
  4.6 0.7 %copy-start.4 = (s32[2]{0:T(128)S(1)}, s32[2]{0:T(128)}, u32[]{:S(2)}) copy-start(s32[2]{0:T(128)} %dims.1) | copy-start | bytes 28

commit v2 on v1

--- a/solution.py
+++ b/solution.py
@@ -15,13 +15,15 @@
 def kernel(
     n_blk,
     n_col,
-    dims,
-    pattern,
+    dims_in,
+    pattern_in,
     psi,
     left_env,
     right_env,
     first_out,
     second_out,
+    dims,
+    pattern,
     raw,
     own,
     near,
@@ -37,6 +39,7 @@
     stat_sum,
     stat_blk,
     local_sem,
+    store_sem,
     near_send,
     near_recv,
     far_send,
@@ -68,6 +71,10 @@
 
     load_psi = pltpu.make_async_copy(psi, raw, local_sem.at[0])
     load_psi.start()
+    load_dims = pltpu.make_async_copy(dims_in, dims, local_sem.at[3])
+    load_dims.start()
+    load_pattern = pltpu.make_async_copy(pattern_in, pattern, local_sem.at[4])
+    load_pattern.start()
     load_left = pltpu.make_async_copy(
         left_env.at[:, :, my_rows, :], left.at[:, pl.ds(c * terms, terms)], local_sem.at[1]
     )
@@ -90,14 +97,18 @@
             barrier, inc=1, device_id=(b, lax.rem(c + k, n_col)), device_id_type=MESH
         )
 
+    load_dims.wait()
+    load_pattern.wait()
     load_psi.wait()
     row_ids = c * rows + lax.broadcasted_iota(jnp.int32, (rows, width), 0)
     col_ids = lax.broadcasted_iota(jnp.int32, (rows, width), 1)
     furthest = jnp.maximum(row_ids, col_ids)
     for s in range(sectors):
-        own[0, s] = jnp.where(
-            furthest < dims[s], raw[s].astype(jnp.float32), 0.0
-        ).astype(jnp.bfloat16)
+        masked_psi = jnp.where(furthest < dims[s], raw[s].astype(jnp.float32), 0.0)
+        for i, (p, r) in enumerate(chunks):
+            own[0, i, s] = masked_psi[
+                r * height : (r + 1) * height, p * LANES : (p + 1) * LANES
+            ].astype(jnp.bfloat16)
 
     @pl.when(jnp.logical_not(has_source))
     def _():
@@ -105,14 +116,10 @@
 
     pl.semaphore_wait(barrier, n_blk + n_col - 2)
 
-    def cut(ref, h, i):
-        p, r = chunks[i]
-        return ref.at[h, :, pl.ds(r * height, height), pl.ds(p * LANES, LANES)]
-
     def to_pair(h, i):
         return pltpu.make_async_remote_copy(
-            src_ref=cut(own, h, i),
-            dst_ref=cut(near, h, i),
+            src_ref=own.at[h, i],
+            dst_ref=near.at[h, i],
             send_sem=near_send.at[h, i],
             recv_sem=near_recv.at[h, i],
             device_id=(pair, c),
@@ -121,8 +128,8 @@
 
     def to_onward(h, i):
         return pltpu.make_async_remote_copy(
-            src_ref=cut(near, h, i),
-            dst_ref=cut(far, h, i),
+            src_ref=near.at[h, i],
+            dst_ref=far.at[h, i],
             send_sem=far_send.at[h, i],
             recv_sem=far_recv.at[h, i],
             device_id=(onward, c),
@@ -132,7 +139,7 @@
     def z_part(h, i, holder):
         p, r = chunks[i]
         start = pl.multiple_of(holder * rows + r * height, 16)
-        return z.at[h, :, pl.ds(start, height), pl.ds(p * LANES, LANES)]
+        return z.at[h, p, :, pl.ds(start, height), :]
 
     def z_copy(h, i, k, holder):
         return pltpu.make_async_remote_copy(
@@ -164,11 +171,8 @@
             )
         ]
 
-    def start_halo(h):
-        for i in range(len(chunks)):
-            to_pair(h, i).start()
-
-    start_halo(0)
+    for i in range(len(chunks)):
+        to_pair(0, i).start()
     for k in range(1, n_col):
         for copy in env_copies(k, c, lax.rem(c + k, n_col)):
             copy.start()
@@ -183,21 +187,20 @@
 
     def combine(h, i, theta):
         p, r = chunks[i]
-        rr, cc = slice(r * height, (r + 1) * height), slice(p * LANES, (p + 1) * LANES)
         start = pl.multiple_of(c * rows + r * height, 16)
         total = [None, None]
         for ref, weights in ((own, inner), (near, near_c), (far, far_c)):
             for k in range(2):
-                block = ref[h, k, rr, cc].astype(jnp.float32)
+                block = ref[h, i, k].astype(jnp.float32)
                 for s in range(2):
                     term = weights[s][k] * block
                     total[s] = term if total[s] is None else total[s] + term
         for s in range(2):
             if h == 0:
-                z_psi[s, rr, cc] = total[s]
+                z_psi[i, s] = total[s]
             else:
-                total[s] = total[s] - theta * z_psi[s, rr, cc]
-            z[h, s, pl.ds(start, height), cc] = total[s].astype(jnp.bfloat16)
+                total[s] = total[s] - theta * z_psi[i, s]
+            z[h, p, s, pl.ds(start, height), :] = total[s].astype(jnp.bfloat16)
 
     def product(h, p):
         cc = slice(p * LANES, (p + 1) * LANES)
@@ -205,7 +208,7 @@
         for s in range(2):
             t = jnp.dot(
                 left[s].reshape(all_terms * rows, width),
-                z[h, s, :, cc],
+                z[h, p, s],
                 preferred_element_type=jnp.float32,
             ).astype(jnp.bfloat16)
             temp.append(t)
@@ -217,13 +220,42 @@
             axis=1,
         )
         weights = jnp.concatenate([right[w, :, cc] for w in range(all_terms)], axis=1)
-        part = lax.dot_general(
-            wide, weights, (((1,), (1,)), ((), ())), preferred_element_type=jnp.float32
-        )
-        if p == 0:
-            acc[...] = part
-        else:
-            acc[...] += part
+        if p < pieces - 1:
+            part = lax.dot_general(
+                wide, weights, (((1,), (1,)), ((), ())), preferred_element_type=jnp.float32
+            )
+            if p == 0:
+                acc[...] = part
+            else:
+                acc[...] += part
+            return
+        for d in range(pieces):
+            dd = slice(d * LANES, (d + 1) * LANES)
+            part = lax.dot_general(
+                wide, weights[dd], (((1,), (1,)), ((), ())), preferred_element_type=jnp.float32
+            )
+            part = (part + acc[:, dd]) * (1.0 / float(all_terms) ** 0.5)
+            for s in range(2):
+                block = jnp.where(
+                    furthest[:, dd] < dims[s], part[s * rows : (s + 1) * rows], 0.0
+                )
+                sig[h, s, :, dd] = block
+                if h == 0:
+                    for r in range(HALVES):
+                        own[1, d * HALVES + r, s] = block[
+                            r * height : (r + 1) * height
+                        ].astype(jnp.bfloat16)
+            if h == 0:
+                for r in range(HALVES):
+                    to_pair(1, d * HALVES + r).start()
+            else:
+                store(1, d).start()
+
+    def store(h, d):
+        dd = pl.ds(d * LANES, LANES)
+        return pltpu.make_async_copy(
+            sig.at[h, :, :, dd], (first_out, second_out)[h].at[:, :, dd], store_sem.at[h, d]
+        )
 
     def finish_piece(h, p):
         for r in range(HALVES):
@@ -237,10 +269,10 @@
                     copy.wait_recv()
         product(h, p)
 
-    def apply(h, theta_of):
+    def apply(h, theta_of, lag):
         theta = None
         count = len(chunks)
-        for i in range(count + 2):
+        for i in range(count + lag + 1):
             if i < count:
                 to_pair(h, i).wait_recv()
 
@@ -248,7 +280,7 @@
                 def _():
                     to_onward(h, i).start()
 
-            j = i - 1
+            j = i - lag
             if 0 <= j < count:
 
                 @pl.when(has_source)
@@ -260,35 +292,22 @@
                 combine(h, j, theta)
                 for k in range(1, n_col):
                     z_copy(h, j, k, c).start()
-            j = i - 2
+            j = i - lag - 1
             if j >= 0 and j % HALVES == HALVES - 1:
                 finish_piece(h, j // HALVES)
 
-    def masked(s):
-        return jnp.where(
-            furthest < dims[s],
-            acc[s * rows : (s + 1) * rows, :] * (1.0 / float(all_terms) ** 0.5),
-            0.0,
-        )
-
-    def fold(x):
-        x = jnp.sum(x.reshape(rows // 8, 8, width), axis=0)
-        out = x[:, :LANES]
-        for p in range(1, pieces):
-            out = out + x[:, p * LANES : (p + 1) * LANES]
-        return out
-
-    apply(0, None)
-    for s in range(2):
-        sig[0, s] = masked(s)
-        own[1, s] = sig[0, s].astype(jnp.bfloat16)
-    start_halo(1)
+    apply(0, None, 1)
     for q in range(2):
         total = None
-        for s in range(2):
-            v = own[0, s].astype(jnp.float32)
-            term = fold(v * (sig[0, s] if q == 0 else v))
-            total = term if total is None else total + term
+        for i, (p, r) in enumerate(chunks):
+            for s in range(2):
+                v = own[0, i, s].astype(jnp.float32)
+                if q == 0:
+                    w = sig[0, s, r * height : (r + 1) * height, p * LANES : (p + 1) * LANES]
+                else:
+                    w = v
+                term = jnp.sum((v * w).reshape(height // 8, 8, LANES), axis=0)
+                total = term if total is None else total + term
         stat_own[q] = total
 
     def stat_to_col(k):
@@ -313,8 +332,8 @@
 
     for k in range(1, n_col):
         stat_to_col(k).start()
-    store_first = pltpu.make_async_copy(sig.at[0], first_out, local_sem.at[3])
-    store_first.start()
+    for d in range(pieces):
+        store(0, d).start()
     for k in range(1, n_col):
         stat_to_col(k).wait_recv()
     total = stat_own[...]
@@ -335,11 +354,7 @@
         sums = [jnp.sum(total[q], axis=(0, 1), keepdims=True) for q in range(2)]
         return sums[0] / sums[1]
 
-    apply(1, theta_of)
-    for s in range(2):
-        sig[1, s] = masked(s)
-    store_second = pltpu.make_async_copy(sig.at[1], second_out, local_sem.at[4])
-    store_second.start()
+    apply(1, theta_of, 3)
 
     for h in range(2):
         for i in range(len(chunks)):
@@ -361,32 +376,35 @@
     def _(i):
         stat_to_blk(i).wait_send()
 
-    store_first.wait()
-    store_second.wait()
+    for h in range(2):
+        for d in range(pieces):
+            store(h, d).wait()
 
 
 def body(n_blk, n_col, psi, dims, pattern, left_env, right_env):
     sectors, rows, width = psi.shape
     terms = left_env.shape[1] * n_col
     chunks = (width // LANES) * HALVES
+    halo = (chunks, sectors, rows // HALVES, LANES)
     bf16, f32 = jnp.bfloat16, jnp.float32
     dma = pltpu.SemaphoreType.DMA
     vmem = pltpu.VMEM
     hbm = pl.BlockSpec(memory_space=pl.ANY)
-    smem = pl.BlockSpec(memory_space=pltpu.SMEM)
     out = jax.ShapeDtypeStruct(psi.shape, f32)
     return pl.pallas_call(
         functools.partial(kernel, n_blk, n_col),
         out_shape=(out, out),
-        in_specs=[smem, smem, hbm, hbm, hbm],
+        in_specs=[hbm] * 5,
         out_specs=(hbm, hbm),
         scratch_shapes=[
+            pltpu.SMEM(dims.shape, jnp.int32),
+            pltpu.SMEM(pattern.shape, jnp.int32),
             vmem((sectors, rows, width), bf16),
-            vmem((2, sectors, rows, width), bf16),
-            vmem((2, sectors, rows, width), bf16),
-            vmem((2, sectors, rows, width), bf16),
-            vmem((2, sectors, width, width), bf16),
-            vmem((sectors, rows, width), f32),
+            vmem((2, *halo), bf16),
+            vmem((2, *halo), bf16),
+            vmem((2, *halo), bf16),
+            vmem((2, width // LANES, sectors, width, LANES), bf16),
+            vmem(halo, f32),
             vmem((sectors, terms, rows, width), bf16),
             vmem((terms, width, width), bf16),
             vmem((sectors * rows, width), f32),
@@ -396,6 +414,7 @@
             vmem((2, 8, LANES), f32),
             vmem((n_blk - 1, 2, 8, LANES), f32),
             dma((5,)),
+            dma((2, width // LANES)),
             dma((2, chunks)),
             dma((2, chunks)),
             dma((2, chunks)),
@@ -410,7 +429,7 @@
             dma((n_blk - 1,)),
         ],
         compiler_params=pltpu.CompilerParams(
-            collective_id=0, has_side_effects=True, vmem_limit_bytes=40 * 1024 * 1024
+            collective_id=0, has_side_effects=True, vmem_limit_bytes=60 * 1024 * 1024
         ),
     )(dims, pattern, psi, left_env, right_env)
 

time: 50.1 us -> 43.1 us (0.86)
  local copies, waits for them, and re-layouts: 6.25 us -> 2.8 us
  Pallas kernels: 42.2 us -> 38.9 us
    unnamed x12 -> x4, local copies, waits for them, and re-layouts: 6.25 us -> 2.8 us
    pallas_call x1, Pallas kernels: 42.2 us -> 38.9 us  [body(): pl.pallas_call(functools.partial(kernel, n_blk, n_col), out_shape=(out, o...]
where the time goes in v2:
time: 43.1 us; the launch traced here: 42.4 us
  Pallas kernels  38.9 us (90%)
  local copies, waits for them, and re-layouts  2.8 us (6%)
  between operations  0.65 us (2%)
    pallas_call x1, Pallas kernels, body(): pl.pallas_call(functools.partial(kernel, n_blk, n_col), out_shape=(out, o...  38.9 us
    unnamed x4, local copies, waits for them, and re-layouts  2.8 us

profile of v2, /device:TPU:7, one launch (start us, length us, event | category | flops | bytes accessed | tf_op | source)
XLA Modules:
  0.0 42.4 jit_solution(469753527234593398)
XLA Ops:
  0.6 38.9 %shard_map.68 = (f32[2,192,384]{2,1,0:T(8,128)}, f32[2,192,384]{2,1,0:T(8,128)}) custom-call(s32[2]{0:T(128)} %dims_in.1, s32[2,5]{1,0:T(2,128)} %pattern_in.1, bf16[2,192,384]{2,1,0:T(8,128)(2,1)} %psi.1, bf16[2,2,384,384]{3,2,1,0:T(8,128)(2,1)} %left_env.1, bf16[2,384,384]{2,1,0:T(8,128)(2,1)} %right_env.1), custom_call_target="tpu_custom_call" | custom-call | tf_op jit(solution)/shard_map/pallas_call | solution.py:394
  39.6 0.0 copy-start
  39.6 2.0 %copy.9 = f32[2,192,384]{2,1,0:T(8,128)} copy(f32[2,192,384]{2,1,0:T(8,128)} %get-tuple-element.4) | data formatting | bytes 1179648
  41.5 0.0 copy-done
  41.5 0.8 %copy.10 = f32[2,192,384]{2,1,0:T(8,128)} copy(f32[2,192,384]{2,1,0:T(8,128)S(1)} %copy-done) | data formatting | bytes 1179648
Async XLA Ops:
  39.6 2.0 %copy-start = (f32[2,192,384]{2,1,0:T(8,128)S(1)}, f32[2,192,384]{2,1,0:T(8,128)}, u32[]{:S(2)}) copy-start(f32[2,192,384]{2,1,0:T(8,128)} %get-tuple-element.5) | copy-start | bytes 1769476

commit v3 on v2

--- a/solution.py
+++ b/solution.py
@@ -9,7 +9,7 @@
 
 MESH = pl.DeviceIdType.MESH
 LANES = 128
-HALVES = 2
+HALVES = 1
 
 
 def kernel(
@@ -354,7 +354,7 @@
         sums = [jnp.sum(total[q], axis=(0, 1), keepdims=True) for q in range(2)]
         return sums[0] / sums[1]
 
-    apply(1, theta_of, 3)
+    apply(1, theta_of, 2)
 
     for h in range(2):
         for i in range(len(chunks)):

time: 43.1 us -> 40.2 us (0.933)
  Pallas kernels: 38.9 us -> 36 us
    pallas_call x1, Pallas kernels: 38.9 us -> 36 us  [body(): pl.pallas_call(functools.partial(kernel, n_blk, n_col), out_shape=(out, o...]
where the time goes in v3:
time: 40.2 us; the launch traced here: 39.4 us
  Pallas kernels  36 us (90%)
  local copies, waits for them, and re-layouts  2.8 us (7%)
  between operations  0.65 us (2%)
    pallas_call x1, Pallas kernels, body(): pl.pallas_call(functools.partial(kernel, n_blk, n_col), out_shape=(out, o...  36 us
    unnamed x4, local copies, waits for them, and re-layouts  2.8 us

profile of v3, /device:TPU:7, one launch (start us, length us, event | category | flops | bytes accessed | tf_op | source)
XLA Modules:
  0.0 39.4 jit_solution(811577195022876074)
XLA Ops:
  0.6 36.0 %shard_map.68 = (f32[2,192,384]{2,1,0:T(8,128)}, f32[2,192,384]{2,1,0:T(8,128)}) custom-call(s32[2]{0:T(128)} %dims_in.1, s32[2,5]{1,0:T(2,128)} %pattern_in.1, bf16[2,192,384]{2,1,0:T(8,128)(2,1)} %psi.1, bf16[2,2,384,384]{3,2,1,0:T(8,128)(2,1)} %left_env.1, bf16[2,384,384]{2,1,0:T(8,128)(2,1)} %right_env.1), custom_call_target="tpu_custom_call" | custom-call | tf_op jit(solution)/shard_map/pallas_call | solution.py:394
  36.6 0.0 copy-start
  36.7 2.0 %copy.9 = f32[2,192,384]{2,1,0:T(8,128)} copy(f32[2,192,384]{2,1,0:T(8,128)} %get-tuple-element.4) | data formatting | bytes 1179648
  38.6 0.0 copy-done
  38.6 0.8 %copy.10 = f32[2,192,384]{2,1,0:T(8,128)} copy(f32[2,192,384]{2,1,0:T(8,128)S(1)} %copy-done) | data formatting | bytes 1179648
Async XLA Ops:
  36.6 2.0 %copy-start = (f32[2,192,384]{2,1,0:T(8,128)S(1)}, f32[2,192,384]{2,1,0:T(8,128)}, u32[]{:S(2)}) copy-start(f32[2,192,384]{2,1,0:T(8,128)} %get-tuple-element.5) | copy-start | bytes 1769476

commit v4 on v3

--- a/solution.py
+++ b/solution.py
@@ -10,6 +10,7 @@
 MESH = pl.DeviceIdType.MESH
 LANES = 128
 HALVES = 1
+PLANE = 4
 
 
 def kernel(
@@ -33,13 +34,11 @@
     left,
     right,
     acc,
-    sig,
     stat_own,
-    stat_col,
+    stat_mate,
     stat_sum,
-    stat_blk,
+    stat_far,
     local_sem,
-    store_sem,
     near_send,
     near_recv,
     far_send,
@@ -48,10 +47,10 @@
     z_recv,
     env_send,
     env_recv,
-    stat_col_send,
-    stat_col_recv,
-    stat_blk_send,
-    stat_blk_recv,
+    stat_mate_send,
+    stat_mate_recv,
+    stat_far_send,
+    stat_far_recv,
 ):
     b = lax.axis_index("blk")
     c = lax.axis_index("col")
@@ -86,16 +85,31 @@
 
     barrier = pltpu.get_barrier_semaphore()
 
-    @pl.loop(1, n_blk)
-    def _(i):
-        pl.semaphore_signal(
-            barrier, inc=1, device_id=(lax.rem(b + i, n_blk), c), device_id_type=MESH
-        )
-
-    for k in range(1, n_col):
-        pl.semaphore_signal(
-            barrier, inc=1, device_id=(b, lax.rem(c + k, n_col)), device_id_type=MESH
-        )
+    planes = n_blk // PLANE
+    plane, place = b // PLANE, lax.rem(b, PLANE)
+    mates = PLANE * n_col
+
+    def mate(m):
+        f = lax.rem(place * n_col + c + m, mates)
+        return (plane * PLANE + f // n_col, lax.rem(f, n_col))
+
+    def beyond(m):
+        return (lax.rem(plane + m, planes) * PLANE + place, c)
+
+    across = jnp.where(place < PLANE // 2, b - 2, b + 2)
+    has_across = (across >= 0) & (across < n_blk)
+
+    @pl.when(has_across)
+    def _():
+        pl.semaphore_signal(barrier, inc=1, device_id=(across, c), device_id_type=MESH)
+
+    @pl.loop(1, planes)
+    def _(m):
+        pl.semaphore_signal(barrier, inc=1, device_id=beyond(m), device_id_type=MESH)
+
+    @pl.loop(1, mates)
+    def _(m):
+        pl.semaphore_signal(barrier, inc=1, device_id=mate(m), device_id_type=MESH)
 
     load_dims.wait()
     load_pattern.wait()
@@ -114,7 +128,7 @@
     def _():
         far[...] = jnp.zeros_like(far)
 
-    pl.semaphore_wait(barrier, n_blk + n_col - 2)
+    pl.semaphore_wait(barrier, mates + planes - 2 + has_across.astype(jnp.int32))
 
     def to_pair(h, i):
         return pltpu.make_async_remote_copy(
@@ -239,7 +253,7 @@
                 block = jnp.where(
                     furthest[:, dd] < dims[s], part[s * rows : (s + 1) * rows], 0.0
                 )
-                sig[h, s, :, dd] = block
+                (first_out, second_out)[h][s, :, dd] = block
                 if h == 0:
                     for r in range(HALVES):
                         own[1, d * HALVES + r, s] = block[
@@ -248,14 +262,6 @@
             if h == 0:
                 for r in range(HALVES):
                     to_pair(1, d * HALVES + r).start()
-            else:
-                store(1, d).start()
-
-    def store(h, d):
-        dd = pl.ds(d * LANES, LANES)
-        return pltpu.make_async_copy(
-            sig.at[h, :, :, dd], (first_out, second_out)[h].at[:, :, dd], store_sem.at[h, d]
-        )
 
     def finish_piece(h, p):
         for r in range(HALVES):
@@ -303,54 +309,53 @@
             for s in range(2):
                 v = own[0, i, s].astype(jnp.float32)
                 if q == 0:
-                    w = sig[0, s, r * height : (r + 1) * height, p * LANES : (p + 1) * LANES]
+                    w = first_out[s, r * height : (r + 1) * height, p * LANES : (p + 1) * LANES]
                 else:
                     w = v
                 term = jnp.sum((v * w).reshape(height // 8, 8, LANES), axis=0)
                 total = term if total is None else total + term
         stat_own[q] = total
 
-    def stat_to_col(k):
+    def stat_to_mate(m):
         return pltpu.make_async_remote_copy(
             src_ref=stat_own,
-            dst_ref=stat_col.at[k - 1],
-            send_sem=stat_col_send.at[k - 1],
-            recv_sem=stat_col_recv.at[k - 1],
-            device_id=(b, lax.rem(c + k, n_col)),
+            dst_ref=stat_mate.at[m - 1],
+            send_sem=stat_mate_send.at[m - 1],
+            recv_sem=stat_mate_recv.at[m - 1],
+            device_id=mate(m),
             device_id_type=MESH,
         )
 
-    def stat_to_blk(i):
+    def stat_beyond(m):
         return pltpu.make_async_remote_copy(
             src_ref=stat_sum,
-            dst_ref=stat_blk.at[i - 1],
-            send_sem=stat_blk_send.at[i - 1],
-            recv_sem=stat_blk_recv.at[i - 1],
-            device_id=(lax.rem(b + i, n_blk), c),
+            dst_ref=stat_far.at[m - 1],
+            send_sem=stat_far_send.at[m - 1],
+            recv_sem=stat_far_recv.at[m - 1],
+            device_id=beyond(m),
             device_id_type=MESH,
         )
 
-    for k in range(1, n_col):
-        stat_to_col(k).start()
-    for d in range(pieces):
-        store(0, d).start()
-    for k in range(1, n_col):
-        stat_to_col(k).wait_recv()
-    total = stat_own[...]
-    for k in range(1, n_col):
-        total = total + stat_col[k - 1]
-    stat_sum[...] = total
-
-    @pl.loop(1, n_blk)
-    def _(i):
-        stat_to_blk(i).start()
+    @pl.loop(1, mates)
+    def _(m):
+        stat_to_mate(m).start()
+
+    @pl.loop(1, mates)
+    def _(m):
+        stat_to_mate(m).wait_recv()
+
+    stat_sum[...] = stat_own[...] + jnp.sum(stat_mate[...], axis=0)
+
+    @pl.loop(1, planes)
+    def _(m):
+        stat_beyond(m).start()
 
     def theta_of():
-        @pl.loop(1, n_blk)
-        def _(i):
-            stat_to_blk(i).wait_recv()
-
-        total = stat_sum[...] + jnp.sum(stat_blk[...], axis=0)
+        @pl.loop(1, planes)
+        def _(m):
+            stat_beyond(m).wait_recv()
+
+        total = stat_sum[...] + jnp.sum(stat_far[...], axis=0)
         sums = [jnp.sum(total[q], axis=(0, 1), keepdims=True) for q in range(2)]
         return sums[0] / sums[1]
 
@@ -370,15 +375,14 @@
     for k in range(1, n_col):
         for copy in env_copies(k, c, lax.rem(c + k, n_col)):
             copy.wait_send()
-        stat_to_col(k).wait_send()
-
-    @pl.loop(1, n_blk)
-    def _(i):
-        stat_to_blk(i).wait_send()
-
-    for h in range(2):
-        for d in range(pieces):
-            store(h, d).wait()
+
+    @pl.loop(1, mates)
+    def _(m):
+        stat_to_mate(m).wait_send()
+
+    @pl.loop(1, planes)
+    def _(m):
+        stat_beyond(m).wait_send()
 
 
 def body(n_blk, n_col, psi, dims, pattern, left_env, right_env):
@@ -386,16 +390,17 @@
     terms = left_env.shape[1] * n_col
     chunks = (width // LANES) * HALVES
     halo = (chunks, sectors, rows // HALVES, LANES)
+    mates, planes = PLANE * n_col, n_blk // PLANE
     bf16, f32 = jnp.bfloat16, jnp.float32
     dma = pltpu.SemaphoreType.DMA
     vmem = pltpu.VMEM
     hbm = pl.BlockSpec(memory_space=pl.ANY)
-    out = jax.ShapeDtypeStruct(psi.shape, f32)
+    out = vmem(psi.shape, f32)
     return pl.pallas_call(
         functools.partial(kernel, n_blk, n_col),
         out_shape=(out, out),
         in_specs=[hbm] * 5,
-        out_specs=(hbm, hbm),
+        out_specs=(pl.BlockSpec(memory_space=vmem),) * 2,
         scratch_shapes=[
             pltpu.SMEM(dims.shape, jnp.int32),
             pltpu.SMEM(pattern.shape, jnp.int32),
@@ -408,13 +413,11 @@
             vmem((sectors, terms, rows, width), bf16),
             vmem((terms, width, width), bf16),
             vmem((sectors * rows, width), f32),
-            vmem((2, sectors, rows, width), f32),
             vmem((2, 8, LANES), f32),
-            vmem((n_col - 1, 2, 8, LANES), f32),
+            vmem((mates - 1, 2, 8, LANES), f32),
             vmem((2, 8, LANES), f32),
-            vmem((n_blk - 1, 2, 8, LANES), f32),
+            vmem((planes - 1, 2, 8, LANES), f32),
             dma((5,)),
-            dma((2, width // LANES)),
             dma((2, chunks)),
             dma((2, chunks)),
             dma((2, chunks)),
@@ -423,10 +426,10 @@
             dma((2, n_col - 1, chunks)),
             dma((n_col - 1, 2)),
             dma((n_col - 1, 2)),
-            dma((n_col - 1,)),
-            dma((n_col - 1,)),
-            dma((n_blk - 1,)),
-            dma((n_blk - 1,)),
+            dma((mates - 1,)),
+            dma((mates - 1,)),
+            dma((planes - 1,)),
+            dma((planes - 1,)),
         ],
         compiler_params=pltpu.CompilerParams(
             collective_id=0, has_side_effects=True, vmem_limit_bytes=60 * 1024 * 1024

time: 40.2 us -> 42.5 us (1.057); the launches traced: 39.4 us -> 42.3 us
  Pallas kernels: 36 us -> 40.1 us
  local copies, waits for them, and re-layouts: 2.8 us -> 1.63 us
    pallas_call x1, Pallas kernels: 36 us -> 40.1 us  [body(): pl.pallas_call(functools.partial(kernel, n_blk, n_col), out_shape=(out, o...]
    unnamed x4 -> x2, local copies, waits for them, and re-layouts: 2.8 us -> 1.63 us
where the time goes in v4:
time: 42.5 us; the launch traced here: 42.3 us
  Pallas kernels  40.1 us (94%)
  local copies, waits for them, and re-layouts  1.63 us (4%)
  between operations  0.64 us (2%)
    pallas_call x1, Pallas kernels, body(): pl.pallas_call(functools.partial(kernel, n_blk, n_col), out_shape=(out, o...  40.1 us
    unnamed x2, local copies, waits for them, and re-layouts  1.63 us

profile of v4, /device:TPU:7, one launch (start us, length us, event | category | flops | bytes accessed | tf_op | source)
XLA Modules:
  0.0 42.3 jit_solution(10545006036783859719)
XLA Ops:
  0.6 40.1 %shard_map.68 = (f32[2,192,384]{2,1,0:T(8,128)S(1)}, f32[2,192,384]{2,1,0:T(8,128)S(1)}) custom-call(s32[2]{0:T(128)} %dims_in.1, s32[2,5]{1,0:T(2,128)} %pattern_in.1, bf16[2,192,384]{2,1,0:T(8,128)(2,1)} %psi.1, bf16[2,2,384,384]{3,2,1,0:T(8,128)(2,1)} %left_env.1, bf16[2,384,384]{2,1,0:T(8,128)(2,1)} %right_env.1), custom_call_target="tpu_custom_call" | custom-call | tf_op jit(solution)/shard_map/pallas_call | solution.py:399
  40.7 0.8 %copy.9 = f32[2,192,384]{2,1,0:T(8,128)} copy(f32[2,192,384]{2,1,0:T(8,128)S(1)} %get-tuple-element.2) | data formatting | bytes 1179648
  41.5 0.8 %copy.10 = f32[2,192,384]{2,1,0:T(8,128)} copy(f32[2,192,384]{2,1,0:T(8,128)S(1)} %get-tuple-element.3) | data formatting | bytes 1179648

commit v5 on v3

--- a/solution.py
+++ b/solution.py
@@ -33,13 +33,11 @@
     left,
     right,
     acc,
-    sig,
     stat_own,
     stat_col,
     stat_sum,
     stat_blk,
     local_sem,
-    store_sem,
     near_send,
     near_recv,
     far_send,
@@ -239,23 +237,14 @@
                 block = jnp.where(
                     furthest[:, dd] < dims[s], part[s * rows : (s + 1) * rows], 0.0
                 )
-                sig[h, s, :, dd] = block
+                (first_out, second_out)[h][s, :, dd] = block
                 if h == 0:
                     for r in range(HALVES):
                         own[1, d * HALVES + r, s] = block[
                             r * height : (r + 1) * height
                         ].astype(jnp.bfloat16)
-            if h == 0:
-                for r in range(HALVES):
-                    to_pair(1, d * HALVES + r).start()
-            else:
-                store(1, d).start()
-
-    def store(h, d):
-        dd = pl.ds(d * LANES, LANES)
-        return pltpu.make_async_copy(
-            sig.at[h, :, :, dd], (first_out, second_out)[h].at[:, :, dd], store_sem.at[h, d]
-        )
+            if h == 0 and d == 0:
+                to_pair(1, 0).start()
 
     def finish_piece(h, p):
         for r in range(HALVES):
@@ -296,19 +285,23 @@
             if j >= 0 and j % HALVES == HALVES - 1:
                 finish_piece(h, j // HALVES)
 
-    apply(0, None, 1)
-    for q in range(2):
+    def inner_product(with_sigma):
         total = None
         for i, (p, r) in enumerate(chunks):
             for s in range(2):
                 v = own[0, i, s].astype(jnp.float32)
-                if q == 0:
-                    w = sig[0, s, r * height : (r + 1) * height, p * LANES : (p + 1) * LANES]
-                else:
-                    w = v
+                w = v
+                if with_sigma:
+                    w = first_out[
+                        s, r * height : (r + 1) * height, p * LANES : (p + 1) * LANES
+                    ]
                 term = jnp.sum((v * w).reshape(height // 8, 8, LANES), axis=0)
                 total = term if total is None else total + term
-        stat_own[q] = total
+        return total
+
+    stat_own[1] = inner_product(False)
+    apply(0, None, 1)
+    stat_own[0] = inner_product(True)
 
     def stat_to_col(k):
         return pltpu.make_async_remote_copy(
@@ -332,8 +325,6 @@
 
     for k in range(1, n_col):
         stat_to_col(k).start()
-    for d in range(pieces):
-        store(0, d).start()
     for k in range(1, n_col):
         stat_to_col(k).wait_recv()
     total = stat_own[...]
@@ -344,6 +335,9 @@
     @pl.loop(1, n_blk)
     def _(i):
         stat_to_blk(i).start()
+
+    for i in range(1, len(chunks)):
+        to_pair(1, i).start()
 
     def theta_of():
         @pl.loop(1, n_blk)
@@ -375,10 +369,6 @@
     @pl.loop(1, n_blk)
     def _(i):
         stat_to_blk(i).wait_send()
-
-    for h in range(2):
-        for d in range(pieces):
-            store(h, d).wait()
 
 
 def body(n_blk, n_col, psi, dims, pattern, left_env, right_env):
@@ -390,12 +380,12 @@
     dma = pltpu.SemaphoreType.DMA
     vmem = pltpu.VMEM
     hbm = pl.BlockSpec(memory_space=pl.ANY)
-    out = jax.ShapeDtypeStruct(psi.shape, f32)
+    out = vmem(psi.shape, f32)
     return pl.pallas_call(
         functools.partial(kernel, n_blk, n_col),
         out_shape=(out, out),
         in_specs=[hbm] * 5,
-        out_specs=(hbm, hbm),
+        out_specs=(pl.BlockSpec(memory_space=vmem),) * 2,
         scratch_shapes=[
             pltpu.SMEM(dims.shape, jnp.int32),
             pltpu.SMEM(pattern.shape, jnp.int32),
@@ -408,13 +398,11 @@
             vmem((sectors, terms, rows, width), bf16),
             vmem((terms, width, width), bf16),
             vmem((sectors * rows, width), f32),
-            vmem((2, sectors, rows, width), f32),
             vmem((2, 8, LANES), f32),
             vmem((n_col - 1, 2, 8, LANES), f32),
             vmem((2, 8, LANES), f32),
             vmem((n_blk - 1, 2, 8, LANES), f32),
             dma((5,)),
-            dma((2, width // LANES)),
             dma((2, chunks)),
             dma((2, chunks)),
             dma((2, chunks)),

time: 40.2 us -> 38.5 us (0.958)
  local copies, waits for them, and re-layouts: 2.8 us -> 1.63 us
    unnamed x4 -> x2, local copies, waits for them, and re-layouts: 2.8 us -> 1.63 us
where the time goes in v5:
time: 38.5 us; the launch traced here: 38 us
  Pallas kernels  35.7 us (93%)
  local copies, waits for them, and re-layouts  1.63 us (4%)
  between operations  0.64 us (2%)
    pallas_call x1, Pallas kernels, body(): pl.pallas_call(functools.partial(kernel, n_blk, n_col), out_shape=(out, o...  35.7 us
    unnamed x2, local copies, waits for them, and re-layouts  1.63 us

profile of v5, /device:TPU:7, one launch (start us, length us, event | category | flops | bytes accessed | tf_op | source)
XLA Modules:
  0.0 38.0 jit_solution(7830739270485478912)
XLA Ops:
  0.6 35.7 %shard_map.68 = (f32[2,192,384]{2,1,0:T(8,128)S(1)}, f32[2,192,384]{2,1,0:T(8,128)S(1)}) custom-call(s32[2]{0:T(128)} %dims_in.1, s32[2,5]{1,0:T(2,128)} %pattern_in.1, bf16[2,192,384]{2,1,0:T(8,128)(2,1)} %psi.1, bf16[2,2,384,384]{3,2,1,0:T(8,128)(2,1)} %left_env.1, bf16[2,384,384]{2,1,0:T(8,128)(2,1)} %right_env.1), custom_call_target="tpu_custom_call" | custom-call | tf_op jit(solution)/shard_map/pallas_call | solution.py:384
  36.3 0.8 %copy.9 = f32[2,192,384]{2,1,0:T(8,128)} copy(f32[2,192,384]{2,1,0:T(8,128)S(1)} %get-tuple-element.2) | data formatting | bytes 1179648
  37.2 0.8 %copy.10 = f32[2,192,384]{2,1,0:T(8,128)} copy(f32[2,192,384]{2,1,0:T(8,128)S(1)} %get-tuple-element.3) | data formatting | bytes 1179648

commit v6 on v5

--- a/solution.py
+++ b/solution.py
@@ -34,9 +34,9 @@
     right,
     acc,
     stat_own,
-    stat_col,
+    stat_mate,
     stat_sum,
-    stat_blk,
+    stat_far,
     local_sem,
     near_send,
     near_recv,
@@ -46,10 +46,7 @@
     z_recv,
     env_send,
     env_recv,
-    stat_col_send,
-    stat_col_recv,
-    stat_blk_send,
-    stat_blk_recv,
+    stat_sem,
 ):
     b = lax.axis_index("blk")
     c = lax.axis_index("col")
@@ -84,16 +81,22 @@
 
     barrier = pltpu.get_barrier_semaphore()
 
-    @pl.loop(1, n_blk)
-    def _(i):
-        pl.semaphore_signal(
-            barrier, inc=1, device_id=(lax.rem(b + i, n_blk), c), device_id_type=MESH
-        )
-
-    for k in range(1, n_col):
-        pl.semaphore_signal(
-            barrier, inc=1, device_id=(b, lax.rem(c + k, n_col)), device_id_type=MESH
-        )
+    side = lax.rem(b, 2)
+    mates, others = 2 * n_col, n_blk // 2
+
+    def mate(m):
+        f = lax.rem(side * n_col + c + m, mates)
+        return (b - side + f // n_col, lax.rem(f, n_col))
+
+    def other(m):
+        return (lax.rem(b + 2 * m, n_blk), c)
+
+    @pl.loop(1, others)
+    def _(m):
+        pl.semaphore_signal(barrier, inc=1, device_id=other(m), device_id_type=MESH)
+
+    for m in range(1, mates):
+        pl.semaphore_signal(barrier, inc=1, device_id=mate(m), device_id_type=MESH)
 
     load_dims.wait()
     load_pattern.wait()
@@ -112,13 +115,13 @@
     def _():
         far[...] = jnp.zeros_like(far)
 
-    pl.semaphore_wait(barrier, n_blk + n_col - 2)
+    pl.semaphore_wait(barrier, mates + others - 2)
 
     def to_pair(h, i):
         return pltpu.make_async_remote_copy(
             src_ref=own.at[h, i],
             dst_ref=near.at[h, i],
-            send_sem=near_send.at[h, i],
+            send_sem=near_send,
             recv_sem=near_recv.at[h, i],
             device_id=(pair, c),
             device_id_type=MESH,
@@ -128,7 +131,7 @@
         return pltpu.make_async_remote_copy(
             src_ref=near.at[h, i],
             dst_ref=far.at[h, i],
-            send_sem=far_send.at[h, i],
+            send_sem=far_send,
             recv_sem=far_recv.at[h, i],
             device_id=(onward, c),
             device_id_type=MESH,
@@ -143,7 +146,7 @@
         return pltpu.make_async_remote_copy(
             src_ref=z_part(h, i, holder),
             dst_ref=z_part(h, i, holder),
-            send_sem=z_send.at[h, k - 1, i],
+            send_sem=z_send.at[k - 1],
             recv_sem=z_recv.at[h, k - 1, i],
             device_id=(b, lax.rem(c + k, n_col)),
             device_id_type=MESH,
@@ -218,33 +221,24 @@
             axis=1,
         )
         weights = jnp.concatenate([right[w, :, cc] for w in range(all_terms)], axis=1)
+        part = lax.dot_general(
+            wide, weights, (((1,), (1,)), ((), ())), preferred_element_type=jnp.float32
+        )
+        if p == 0:
+            acc[...] = part
+            return
         if p < pieces - 1:
-            part = lax.dot_general(
-                wide, weights, (((1,), (1,)), ((), ())), preferred_element_type=jnp.float32
-            )
-            if p == 0:
-                acc[...] = part
-            else:
-                acc[...] += part
+            acc[...] += part
             return
-        for d in range(pieces):
-            dd = slice(d * LANES, (d + 1) * LANES)
-            part = lax.dot_general(
-                wide, weights[dd], (((1,), (1,)), ((), ())), preferred_element_type=jnp.float32
-            )
-            part = (part + acc[:, dd]) * (1.0 / float(all_terms) ** 0.5)
-            for s in range(2):
-                block = jnp.where(
-                    furthest[:, dd] < dims[s], part[s * rows : (s + 1) * rows], 0.0
-                )
-                (first_out, second_out)[h][s, :, dd] = block
-                if h == 0:
-                    for r in range(HALVES):
-                        own[1, d * HALVES + r, s] = block[
-                            r * height : (r + 1) * height
-                        ].astype(jnp.bfloat16)
-            if h == 0 and d == 0:
-                to_pair(1, 0).start()
+        part = (part + acc[...]) * (1.0 / float(all_terms) ** 0.5)
+        for s in range(2):
+            block = jnp.where(furthest < dims[s], part[s * rows : (s + 1) * rows], 0.0)
+            (first_out, second_out)[h][s] = block
+            if h == 0:
+                for i, (q, r) in enumerate(chunks):
+                    own[1, i, s] = block[
+                        r * height : (r + 1) * height, q * LANES : (q + 1) * LANES
+                    ].astype(jnp.bfloat16)
 
     def finish_piece(h, p):
         for r in range(HALVES):
@@ -284,6 +278,9 @@
             j = i - lag - 1
             if j >= 0 and j % HALVES == HALVES - 1:
                 finish_piece(h, j // HALVES)
+
+    def settle(ref, sem):
+        pltpu.make_async_copy(ref, ref, sem).wait()
 
     def inner_product(with_sigma):
         total = None
@@ -303,72 +300,57 @@
     apply(0, None, 1)
     stat_own[0] = inner_product(True)
 
-    def stat_to_col(k):
+    def stat_to_mate(m):
         return pltpu.make_async_remote_copy(
             src_ref=stat_own,
-            dst_ref=stat_col.at[k - 1],
-            send_sem=stat_col_send.at[k - 1],
-            recv_sem=stat_col_recv.at[k - 1],
-            device_id=(b, lax.rem(c + k, n_col)),
+            dst_ref=stat_mate.at[m - 1],
+            send_sem=stat_sem.at[0],
+            recv_sem=stat_sem.at[1],
+            device_id=mate(m),
             device_id_type=MESH,
         )
 
-    def stat_to_blk(i):
+    def stat_to_other(m):
         return pltpu.make_async_remote_copy(
             src_ref=stat_sum,
-            dst_ref=stat_blk.at[i - 1],
-            send_sem=stat_blk_send.at[i - 1],
-            recv_sem=stat_blk_recv.at[i - 1],
-            device_id=(lax.rem(b + i, n_blk), c),
+            dst_ref=stat_far.at[m - 1],
+            send_sem=stat_sem.at[2],
+            recv_sem=stat_sem.at[3],
+            device_id=other(m),
             device_id_type=MESH,
         )
 
-    for k in range(1, n_col):
-        stat_to_col(k).start()
-    for k in range(1, n_col):
-        stat_to_col(k).wait_recv()
-    total = stat_own[...]
-    for k in range(1, n_col):
-        total = total + stat_col[k - 1]
-    stat_sum[...] = total
-
-    @pl.loop(1, n_blk)
-    def _(i):
-        stat_to_blk(i).start()
-
-    for i in range(1, len(chunks)):
+    for m in range(1, mates):
+        stat_to_mate(m).start()
+    for i in range(len(chunks)):
         to_pair(1, i).start()
+    settle(stat_mate, stat_sem.at[1])
+    stat_sum[...] = stat_own[...] + jnp.sum(stat_mate[...], axis=0)
+
+    @pl.loop(1, others)
+    def _(m):
+        stat_to_other(m).start()
 
     def theta_of():
-        @pl.loop(1, n_blk)
-        def _(i):
-            stat_to_blk(i).wait_recv()
-
-        total = stat_sum[...] + jnp.sum(stat_blk[...], axis=0)
+        settle(stat_far, stat_sem.at[3])
+        total = stat_sum[...] + jnp.sum(stat_far[...], axis=0)
         sums = [jnp.sum(total[q], axis=(0, 1), keepdims=True) for q in range(2)]
         return sums[0] / sums[1]
 
-    apply(1, theta_of, 2)
-
-    for h in range(2):
-        for i in range(len(chunks)):
-            to_pair(h, i).wait_send()
-            for k in range(1, n_col):
-                z_copy(h, i, k, c).wait_send()
-
-        @pl.when(has_onward)
-        def _():
-            for i in range(len(chunks)):
-                to_onward(h, i).wait_send()
+    apply(1, theta_of, 1)
+
+    settle(stat_mate, stat_sem.at[0])
+    settle(stat_far, stat_sem.at[2])
+    settle(own, near_send)
+
+    @pl.when(has_onward)
+    def _():
+        settle(near, far_send)
 
     for k in range(1, n_col):
+        settle(own, z_send.at[k - 1])
         for copy in env_copies(k, c, lax.rem(c + k, n_col)):
             copy.wait_send()
-        stat_to_col(k).wait_send()
-
-    @pl.loop(1, n_blk)
-    def _(i):
-        stat_to_blk(i).wait_send()
 
 
 def body(n_blk, n_col, psi, dims, pattern, left_env, right_env):
@@ -399,22 +381,19 @@
             vmem((terms, width, width), bf16),
             vmem((sectors * rows, width), f32),
             vmem((2, 8, LANES), f32),
-            vmem((n_col - 1, 2, 8, LANES), f32),
+            vmem((2 * n_col - 1, 2, 8, LANES), f32),
             vmem((2, 8, LANES), f32),
-            vmem((n_blk - 1, 2, 8, LANES), f32),
+            vmem((n_blk // 2 - 1, 2, 8, LANES), f32),
             dma((5,)),
+            dma(()),
             dma((2, chunks)),
+            dma(()),
             dma((2, chunks)),
-            dma((2, chunks)),
-            dma((2, chunks)),
-            dma((2, n_col - 1, chunks)),
+            dma((n_col - 1,)),
             dma((2, n_col - 1, chunks)),
             dma((n_col - 1, 2)),
             dma((n_col - 1, 2)),
-            dma((n_col - 1,)),
-            dma((n_col - 1,)),
-            dma((n_blk - 1,)),
-            dma((n_blk - 1,)),
+            dma((4,)),
         ],
         compiler_params=pltpu.CompilerParams(
             collective_id=0, has_side_effects=True, vmem_limit_bytes=60 * 1024 * 1024

time: 38.5 us -> 37.1 us (0.964)
  Pallas kernels: 35.7 us -> 34.5 us
    pallas_call x1, Pallas kernels: 35.7 us -> 34.5 us  [body(): pl.pallas_call(functools.partial(kernel, n_blk, n_col), out_shape=(out, o...]
where the time goes in v6:
time: 37.1 us; the launch traced here: 36.8 us
  Pallas kernels  34.5 us (93%)
  local copies, waits for them, and re-layouts  1.63 us (4%)
  between operations  0.64 us (2%)
    pallas_call x1, Pallas kernels, body(): pl.pallas_call(functools.partial(kernel, n_blk, n_col), out_shape=(out, o...  34.5 us
    unnamed x2, local copies, waits for them, and re-layouts  1.63 us

profile of v6, /device:TPU:7, one launch (start us, length us, event | category | flops | bytes accessed | tf_op | source)
XLA Modules:
  0.0 36.8 jit_solution(7013391624474275078)
XLA Ops:
  0.6 34.5 %shard_map.68 = (f32[2,192,384]{2,1,0:T(8,128)S(1)}, f32[2,192,384]{2,1,0:T(8,128)S(1)}) custom-call(s32[2]{0:T(128)} %dims_in.1, s32[2,5]{1,0:T(2,128)} %pattern_in.1, bf16[2,192,384]{2,1,0:T(8,128)(2,1)} %psi.1, bf16[2,2,384,384]{3,2,1,0:T(8,128)(2,1)} %left_env.1, bf16[2,384,384]{2,1,0:T(8,128)(2,1)} %right_env.1), custom_call_target="tpu_custom_call" | custom-call | tf_op jit(solution)/shard_map/pallas_call | solution.py:366
  35.2 0.8 %copy.9 = f32[2,192,384]{2,1,0:T(8,128)} copy(f32[2,192,384]{2,1,0:T(8,128)S(1)} %get-tuple-element.2) | data formatting | bytes 1179648
  36.0 0.8 %copy.10 = f32[2,192,384]{2,1,0:T(8,128)} copy(f32[2,192,384]{2,1,0:T(8,128)S(1)} %get-tuple-element.3) | data formatting | bytes 1179648

commit v7 on v6

--- a/solution.py
+++ b/solution.py
@@ -32,6 +32,7 @@
     z_psi,
     left,
     right,
+    turned,
     acc,
     stat_own,
     stat_mate,
@@ -204,7 +205,6 @@
             z[h, p, s, pl.ds(start, height), :] = total[s].astype(jnp.bfloat16)
 
     def product(h, p):
-        cc = slice(p * LANES, (p + 1) * LANES)
         temp = []
         for s in range(2):
             t = jnp.dot(
@@ -220,10 +220,7 @@
             ],
             axis=1,
         )
-        weights = jnp.concatenate([right[w, :, cc] for w in range(all_terms)], axis=1)
-        part = lax.dot_general(
-            wide, weights, (((1,), (1,)), ((), ())), preferred_element_type=jnp.float32
-        )
+        part = jnp.dot(wide, turned[p], preferred_element_type=jnp.float32)
         if p == 0:
             acc[...] = part
             return
@@ -244,13 +241,19 @@
         for r in range(HALVES):
             for k in range(1, n_col):
                 z_copy(h, p * HALVES + r, k, lax.rem(c + n_col - k, n_col)).wait_recv()
-        if h == 0 and p == 0:
-            load_left.wait()
-            load_right.wait()
-            for k in range(1, n_col):
-                for copy in env_copies(k, lax.rem(c + n_col - k, n_col), c):
-                    copy.wait_recv()
         product(h, p)
+
+    def settle_env():
+        load_left.wait()
+        load_right.wait()
+        for k in range(1, n_col):
+            for copy in env_copies(k, lax.rem(c + n_col - k, n_col), c):
+                copy.wait_recv()
+        for p in range(pieces):
+            for w in range(all_terms):
+                turned[p, w * LANES : (w + 1) * LANES, :] = right[
+                    w, :, p * LANES : (p + 1) * LANES
+                ].T
 
     def apply(h, theta_of, lag):
         theta = None
@@ -262,6 +265,9 @@
                 @pl.when(has_onward)
                 def _():
                     to_onward(h, i).start()
+
+                if h == 0 and i == 0:
+                    settle_env()
 
             j = i - lag
             if 0 <= j < count:
@@ -353,6 +359,17 @@
             copy.wait_send()
 
 
+def write_out(first, second, first_out, second_out, sem):
+    copies = [
+        pltpu.make_async_copy(first, first_out, sem.at[0]),
+        pltpu.make_async_copy(second, second_out, sem.at[1]),
+    ]
+    for copy in copies:
+        copy.start()
+    for copy in copies:
+        copy.wait()
+
+
 def body(n_blk, n_col, psi, dims, pattern, left_env, right_env):
     sectors, rows, width = psi.shape
     terms = left_env.shape[1] * n_col
@@ -363,7 +380,7 @@
     vmem = pltpu.VMEM
     hbm = pl.BlockSpec(memory_space=pl.ANY)
     out = vmem(psi.shape, f32)
-    return pl.pallas_call(
+    first, second = pl.pallas_call(
         functools.partial(kernel, n_blk, n_col),
         out_shape=(out, out),
         in_specs=[hbm] * 5,
@@ -379,6 +396,7 @@
             vmem(halo, f32),
             vmem((sectors, terms, rows, width), bf16),
             vmem((terms, width, width), bf16),
+            vmem((width // LANES, terms * LANES, width), bf16),
             vmem((sectors * rows, width), f32),
             vmem((2, 8, LANES), f32),
             vmem((2 * n_col - 1, 2, 8, LANES), f32),
@@ -399,6 +417,14 @@
             collective_id=0, has_side_effects=True, vmem_limit_bytes=60 * 1024 * 1024
         ),
     )(dims, pattern, psi, left_env, right_env)
+    out = jax.ShapeDtypeStruct(psi.shape, f32)
+    return pl.pallas_call(
+        write_out,
+        out_shape=(out, out),
+        in_specs=[pl.BlockSpec(memory_space=vmem)] * 2,
+        out_specs=(hbm, hbm),
+        scratch_shapes=[dma((2,))],
+    )(first, second)
 
 
 def solution(mesh):

time: 37.1 us -> 39.4 us (1.062)
  Pallas kernels: 34.5 us -> 36.8 us
    pallas_call x0 -> x1, Pallas kernels: none -> 2.27 us  [body(): pl.pallas_call(write_out, out_shape=(out, out), in_specs=[pl.BlockSpec(me...]
    unnamed x2 -> x4, local copies, waits for them, and re-layouts: 1.63 us -> 1.61 us
where the time goes in v7:
time: 39.4 us; the launch traced here: 39 us
  Pallas kernels  36.8 us (93%)
  local copies, waits for them, and re-layouts  1.61 us (4%)
  between operations  0.65 us (2%)
    pallas_call x1, Pallas kernels, body(): pl.pallas_call(functools.partial(kernel, n_blk, n_col), out_shape=(out, o...  34.5 us
    pallas_call x1, Pallas kernels, body(): pl.pallas_call(write_out, out_shape=(out, out), in_specs=[pl.BlockSpec(me...  2.27 us
    unnamed x4, local copies, waits for them, and re-layouts  1.61 us

profile of v7, /device:TPU:7, one launch (start us, length us, event | category | flops | bytes accessed | tf_op | source)
XLA Modules:
  0.0 39.0 jit_solution(9075699317165145811)
XLA Ops:
  0.6 34.5 %shard_map.68 = (f32[2,192,384]{2,1,0:T(8,128)S(1)}, f32[2,192,384]{2,1,0:T(8,128)S(1)}) custom-call(s32[2]{0:T(128)} %dims_in.1, s32[2,5]{1,0:T(2,128)} %pattern_in.1, bf16[2,192,384]{2,1,0:T(8,128)(2,1)} %psi.1, bf16[2,2,384,384]{3,2,1,0:T(8,128)(2,1)} %left_env.1, bf16[2,384,384]{2,1,0:T(8,128)(2,1)} %right_env.1), custom_call_target="tpu_custom_call" | custom-call | tf_op jit(solution)/shard_map/pallas_call | solution.py:383
  35.2 0.0 copy-start
  35.2 0.8 %copy-done = f32[2,192,384]{2,1,0:T(8,128)} copy-done((f32[2,192,384]{2,1,0:T(8,128)}, f32[2,192,384]{2,1,0:T(8,128)S(1)}, u32[]{:S(2)}) %copy-start) | copy-done | bytes 589848
  36.0 0.0 copy-start.1
  36.0 0.8 %copy-done.1 = f32[2,192,384]{2,1,0:T(8,128)} copy-done((f32[2,192,384]{2,1,0:T(8,128)}, f32[2,192,384]{2,1,0:T(8,128)S(1)}, u32[]{:S(2)}) %copy-start.1) | copy-done | bytes 589848
  36.8 2.3 %shard_map.69 = (f32[2,192,384]{2,1,0:T(8,128)}, f32[2,192,384]{2,1,0:T(8,128)}) custom-call(f32[2,192,384]{2,1,0:T(8,128)} %copy-done, f32[2,192,384]{2,1,0:T(8,128)} %copy-done.1), custom_call_target="tpu_custom_call" | custom-call | tf_op jit(solution)/shard_map/pallas_call | solution.py:421
Async XLA Ops:
  35.2 0.8 %copy-start = (f32[2,192,384]{2,1,0:T(8,128)}, f32[2,192,384]{2,1,0:T(8,128)S(1)}, u32[]{:S(2)}) copy-start(f32[2,192,384]{2,1,0:T(8,128)S(1)} %get-tuple-element.4.first) | copy-start | bytes 1769476
  36.0 0.8 %copy-start.1 = (f32[2,192,384]{2,1,0:T(8,128)}, f32[2,192,384]{2,1,0:T(8,128)S(1)}, u32[]{:S(2)}) copy-start(f32[2,192,384]{2,1,0:T(8,128)S(1)} %get-tuple-element.5.second) | copy-start | bytes 1769476

commit v8 on v7

--- a/solution.py
+++ b/solution.py
@@ -43,6 +43,8 @@
     near_recv,
     far_send,
     far_recv,
+    direct_send,
+    direct_recv,
     z_send,
     z_recv,
     env_send,
@@ -56,12 +58,14 @@
     all_terms = terms * n_col
     pieces = width // LANES
     height = rows // HALVES
+    last = pieces * HALVES - 1
     chunks = [(p, r) for p in range(pieces) for r in range(HALVES)]
     even = lax.rem(b, 2) == 0
     pair = b + 1 - 2 * lax.rem(b, 2)
     onward = b + 2 - 4 * lax.rem(b, 2)
     source = b - 2 + 4 * lax.rem(b, 2)
     has_onward = (onward >= 0) & (onward < n_blk)
+    opposite = b - 1 + 2 * lax.rem(b, 2)
     has_source = (source >= 0) & (source < n_blk)
     my_rows = pl.ds(pl.multiple_of(c * rows, 16), rows)
 
@@ -92,6 +96,10 @@
     def other(m):
         return (lax.rem(b + 2 * m, n_blk), c)
 
+    @pl.when(has_source)
+    def _():
+        pl.semaphore_signal(barrier, inc=1, device_id=(opposite, c), device_id_type=MESH)
+
     @pl.loop(1, others)
     def _(m):
         pl.semaphore_signal(barrier, inc=1, device_id=other(m), device_id_type=MESH)
@@ -116,7 +124,7 @@
     def _():
         far[...] = jnp.zeros_like(far)
 
-    pl.semaphore_wait(barrier, mates + others - 2)
+    pl.semaphore_wait(barrier, mates + others - 2 + has_source.astype(jnp.int32))
 
     def to_pair(h, i):
         return pltpu.make_async_remote_copy(
@@ -129,14 +137,35 @@
         )
 
     def to_onward(h, i):
-        return pltpu.make_async_remote_copy(
-            src_ref=near.at[h, i],
-            dst_ref=far.at[h, i],
-            send_sem=far_send,
+        count = rows // 2 if i == last else rows
+        part = pl.ds(0, count)
+        return pltpu.make_async_remote_copy(
+            src_ref=near.at[h, i, :, part],
+            dst_ref=far.at[h, i, :, part],
+            send_sem=far_send.at[h, i],
             recv_sem=far_recv.at[h, i],
             device_id=(onward, c),
             device_id_type=MESH,
         )
+
+    def direct(h):
+        part = pl.ds(rows // 2, rows - rows // 2)
+        return pltpu.make_async_remote_copy(
+            src_ref=own.at[h, last, :, part],
+            dst_ref=far.at[h, last, :, part],
+            send_sem=direct_send.at[h],
+            recv_sem=direct_recv.at[h],
+            device_id=(opposite, c),
+            device_id_type=MESH,
+        )
+
+    def start_halo(h):
+        for i in range(len(chunks)):
+            to_pair(h, i).start()
+
+        @pl.when(has_source)
+        def _():
+            direct(h).start()
 
     def z_part(h, i, holder):
         p, r = chunks[i]
@@ -173,8 +202,7 @@
             )
         ]
 
-    for i in range(len(chunks)):
-        to_pair(0, i).start()
+    start_halo(0)
     for k in range(1, n_col):
         for copy in env_copies(k, c, lax.rem(c + k, n_col)):
             copy.start()
@@ -275,6 +303,8 @@
                 @pl.when(has_source)
                 def _():
                     to_onward(h, j).wait_recv()
+                    if j == last:
+                        direct(h).wait_recv()
 
                 if j == 0 and theta_of is not None:
                     theta = theta_of()
@@ -328,8 +358,7 @@
 
     for m in range(1, mates):
         stat_to_mate(m).start()
-    for i in range(len(chunks)):
-        to_pair(1, i).start()
+    start_halo(1)
     settle(stat_mate, stat_sem.at[1])
     stat_sum[...] = stat_own[...] + jnp.sum(stat_mate[...], axis=0)
 
@@ -351,23 +380,19 @@
 
     @pl.when(has_onward)
     def _():
-        settle(near, far_send)
+        for h in range(2):
+            for i in range(len(chunks)):
+                to_onward(h, i).wait_send()
+
+    @pl.when(has_source)
+    def _():
+        for h in range(2):
+            direct(h).wait_send()
 
     for k in range(1, n_col):
         settle(own, z_send.at[k - 1])
         for copy in env_copies(k, c, lax.rem(c + k, n_col)):
             copy.wait_send()
-
-
-def write_out(first, second, first_out, second_out, sem):
-    copies = [
-        pltpu.make_async_copy(first, first_out, sem.at[0]),
-        pltpu.make_async_copy(second, second_out, sem.at[1]),
-    ]
-    for copy in copies:
-        copy.start()
-    for copy in copies:
-        copy.wait()
 
 
 def body(n_blk, n_col, psi, dims, pattern, left_env, right_env):
@@ -380,7 +405,7 @@
     vmem = pltpu.VMEM
     hbm = pl.BlockSpec(memory_space=pl.ANY)
     out = vmem(psi.shape, f32)
-    first, second = pl.pallas_call(
+    return pl.pallas_call(
         functools.partial(kernel, n_blk, n_col),
         out_shape=(out, out),
         in_specs=[hbm] * 5,
@@ -405,8 +430,10 @@
             dma((5,)),
             dma(()),
             dma((2, chunks)),
-            dma(()),
             dma((2, chunks)),
+            dma((2, chunks)),
+            dma((2,)),
+            dma((2,)),
             dma((n_col - 1,)),
             dma((2, n_col - 1, chunks)),
             dma((n_col - 1, 2)),
@@ -417,14 +444,6 @@
             collective_id=0, has_side_effects=True, vmem_limit_bytes=60 * 1024 * 1024
         ),
     )(dims, pattern, psi, left_env, right_env)
-    out = jax.ShapeDtypeStruct(psi.shape, f32)
-    return pl.pallas_call(
-        write_out,
-        out_shape=(out, out),
-        in_specs=[pl.BlockSpec(memory_space=vmem)] * 2,
-        out_specs=(hbm, hbm),
-        scratch_shapes=[dma((2,))],
-    )(first, second)
 
 
 def solution(mesh):

time: 39.4 us -> 38.6 us (0.980)
  Pallas kernels: 36.8 us -> 35.6 us
    pallas_call x1 -> x0, Pallas kernels: 2.27 us -> none  [body(): pl.pallas_call(write_out, out_shape=(out, out), in_specs=[pl.BlockSpec(me...]
    pallas_call x1, Pallas kernels: 34.5 us -> 35.6 us  [body(): pl.pallas_call(functools.partial(kernel, n_blk, n_col), out_shape=(out, o...]
    unnamed x4 -> x2, local copies, waits for them, and re-layouts: 1.61 us -> 1.63 us
where the time goes in v8:
time: 38.6 us; the launch traced here: 37.9 us
  Pallas kernels  35.6 us (92%)
  local copies, waits for them, and re-layouts  1.63 us (4%)
  between operations  0.64 us (2%)
    pallas_call x1, Pallas kernels, body(): pl.pallas_call(functools.partial(kernel, n_blk, n_col), out_shape=(out, o...  35.6 us
    unnamed x2, local copies, waits for them, and re-layouts  1.63 us

profile of v8, /device:TPU:7, one launch (start us, length us, event | category | flops | bytes accessed | tf_op | source)
XLA Modules:
  0.0 37.9 jit_solution(8596464669641209795)
XLA Ops:
  0.6 35.6 %shard_map.68 = (f32[2,192,384]{2,1,0:T(8,128)S(1)}, f32[2,192,384]{2,1,0:T(8,128)S(1)}) custom-call(s32[2]{0:T(128)} %dims_in.1, s32[2,5]{1,0:T(2,128)} %pattern_in.1, bf16[2,192,384]{2,1,0:T(8,128)(2,1)} %psi.1, bf16[2,2,384,384]{3,2,1,0:T(8,128)(2,1)} %left_env.1, bf16[2,384,384]{2,1,0:T(8,128)(2,1)} %right_env.1), custom_call_target="tpu_custom_call" | custom-call | tf_op jit(solution)/shard_map/pallas_call | solution.py:408
  36.2 0.8 %copy.9 = f32[2,192,384]{2,1,0:T(8,128)} copy(f32[2,192,384]{2,1,0:T(8,128)S(1)} %get-tuple-element.2) | data formatting | bytes 1179648
  37.1 0.8 %copy.10 = f32[2,192,384]{2,1,0:T(8,128)} copy(f32[2,192,384]{2,1,0:T(8,128)S(1)} %get-tuple-element.3) | data formatting | bytes 1179648

commit v9 on v7

--- a/solution.py
+++ b/solution.py
@@ -30,6 +30,7 @@
     far,
     z,
     z_psi,
+    early,
     left,
     right,
     turned,
@@ -187,16 +188,28 @@
     near_c = [[jnp.where(even, above[s][k], below[s][k]) for k in range(2)] for s in range(2)]
     far_c = [[jnp.where(even, below[s][k], above[s][k]) for k in range(2)] for s in range(2)]
 
-    def combine(h, i, theta):
-        p, r = chunks[i]
-        start = pl.multiple_of(c * rows + r * height, 16)
-        total = [None, None]
-        for ref, weights in ((own, inner), (near, near_c), (far, far_c)):
+    def weigh(h, i, parts, total):
+        for ref, weights in parts:
             for k in range(2):
                 block = ref[h, i, k].astype(jnp.float32)
                 for s in range(2):
                     term = weights[s][k] * block
                     total[s] = term if total[s] is None else total[s] + term
+        return total
+
+    def combine_near(h, i):
+        total = weigh(h, i, ((own, inner), (near, near_c)), [None, None])
+        for s in range(2):
+            if h == 1:
+                early[i, s] = total[s]
+            else:
+                z_psi[i, s] = total[s]
+
+    def combine(h, i, theta):
+        p, r = chunks[i]
+        start = pl.multiple_of(c * rows + r * height, 16)
+        ref = early if h == 1 else z_psi
+        total = weigh(h, i, ((far, far_c),), [ref[i, s] for s in range(2)])
         for s in range(2):
             if h == 0:
                 z_psi[i, s] = total[s]
@@ -266,7 +279,8 @@
                 def _():
                     to_onward(h, i).start()
 
-                if h == 0 and i == 0:
+                combine_near(h, i)
+                if h == 0 and i == 1:
                     settle_env()
 
             j = i - lag
@@ -283,6 +297,8 @@
                     z_copy(h, j, k, c).start()
             j = i - lag - 1
             if j >= 0 and j % HALVES == HALVES - 1:
+                if h == 1 and j == count - 1:
+                    settle_sends()
                 finish_piece(h, j // HALVES)
 
     def settle(ref, sem):
@@ -343,31 +359,22 @@
         sums = [jnp.sum(total[q], axis=(0, 1), keepdims=True) for q in range(2)]
         return sums[0] / sums[1]
 
-    apply(1, theta_of, 1)
-
-    settle(stat_mate, stat_sem.at[0])
-    settle(stat_far, stat_sem.at[2])
-    settle(own, near_send)
-
-    @pl.when(has_onward)
-    def _():
-        settle(near, far_send)
-
+    def settle_sends():
+        settle(stat_mate, stat_sem.at[0])
+        settle(stat_far, stat_sem.at[2])
+        settle(own, near_send)
+
+        @pl.when(has_onward)
+        def _():
+            settle(near, far_send)
+
+        for k in range(1, n_col):
+            for copy in env_copies(k, c, lax.rem(c + k, n_col)):
+                copy.wait_send()
+
+    apply(1, theta_of, 2)
     for k in range(1, n_col):
         settle(own, z_send.at[k - 1])
-        for copy in env_copies(k, c, lax.rem(c + k, n_col)):
-            copy.wait_send()
-
-
-def write_out(first, second, first_out, second_out, sem):
-    copies = [
-        pltpu.make_async_copy(first, first_out, sem.at[0]),
-        pltpu.make_async_copy(second, second_out, sem.at[1]),
-    ]
-    for copy in copies:
-        copy.start()
-    for copy in copies:
-        copy.wait()
 
 
 def body(n_blk, n_col, psi, dims, pattern, left_env, right_env):
@@ -380,7 +387,7 @@
     vmem = pltpu.VMEM
     hbm = pl.BlockSpec(memory_space=pl.ANY)
     out = vmem(psi.shape, f32)
-    first, second = pl.pallas_call(
+    return pl.pallas_call(
         functools.partial(kernel, n_blk, n_col),
         out_shape=(out, out),
         in_specs=[hbm] * 5,
@@ -393,6 +400,7 @@
             vmem((2, *halo), bf16),
             vmem((2, *halo), bf16),
             vmem((2, width // LANES, sectors, width, LANES), bf16),
+            vmem(halo, f32),
             vmem(halo, f32),
             vmem((sectors, terms, rows, width), bf16),
             vmem((terms, width, width), bf16),
@@ -417,14 +425,6 @@
             collective_id=0, has_side_effects=True, vmem_limit_bytes=60 * 1024 * 1024
         ),
     )(dims, pattern, psi, left_env, right_env)
-    out = jax.ShapeDtypeStruct(psi.shape, f32)
-    return pl.pallas_call(
-        write_out,
-        out_shape=(out, out),
-        in_specs=[pl.BlockSpec(memory_space=vmem)] * 2,
-        out_specs=(hbm, hbm),
-        scratch_shapes=[dma((2,))],
-    )(first, second)
 
 
 def solution(mesh):

time: 39.4 us -> 36.8 us (0.934)
  Pallas kernels: 36.8 us -> 34.3 us
    pallas_call x1 -> x0, Pallas kernels: 2.27 us -> none  [body(): pl.pallas_call(write_out, out_shape=(out, out), in_specs=[pl.BlockSpec(me...]
    unnamed x4 -> x2, local copies, waits for them, and re-layouts: 1.61 us -> 1.63 us
where the time goes in v9:
time: 36.8 us; the launch traced here: 36.6 us
  Pallas kernels  34.3 us (93%)
  local copies, waits for them, and re-layouts  1.63 us (4%)
  between operations  0.64 us (2%)
    pallas_call x1, Pallas kernels, body(): pl.pallas_call(functools.partial(kernel, n_blk, n_col), out_shape=(out, o...  34.3 us
    unnamed x2, local copies, waits for them, and re-layouts  1.63 us

profile of v9, /device:TPU:7, one launch (start us, length us, event | category | flops | bytes accessed | tf_op | source)
XLA Modules:
  0.0 36.6 jit_solution(13187108208709846578)
XLA Ops:
  0.6 34.3 %shard_map.68 = (f32[2,192,384]{2,1,0:T(8,128)S(1)}, f32[2,192,384]{2,1,0:T(8,128)S(1)}) custom-call(s32[2]{0:T(128)} %dims_in.1, s32[2,5]{1,0:T(2,128)} %pattern_in.1, bf16[2,192,384]{2,1,0:T(8,128)(2,1)} %psi.1, bf16[2,2,384,384]{3,2,1,0:T(8,128)(2,1)} %left_env.1, bf16[2,384,384]{2,1,0:T(8,128)(2,1)} %right_env.1), custom_call_target="tpu_custom_call" | custom-call | tf_op jit(solution)/shard_map/pallas_call | solution.py:390
  35.0 0.8 %copy.9 = f32[2,192,384]{2,1,0:T(8,128)} copy(f32[2,192,384]{2,1,0:T(8,128)S(1)} %get-tuple-element.2) | data formatting | bytes 1179648
  35.8 0.8 %copy.10 = f32[2,192,384]{2,1,0:T(8,128)} copy(f32[2,192,384]{2,1,0:T(8,128)S(1)} %get-tuple-element.3) | data formatting | bytes 1179648

commit v10 on v9

--- a/solution.py
+++ b/solution.py
@@ -9,7 +9,7 @@
 
 MESH = pl.DeviceIdType.MESH
 LANES = 128
-HALVES = 1
+HALVES = 2
 
 
 def kernel(
@@ -280,7 +280,7 @@
                     to_onward(h, i).start()
 
                 combine_near(h, i)
-                if h == 0 and i == 1:
+                if h == 0 and i == 2 * HALVES - 1:
                     settle_env()
 
             j = i - lag
@@ -372,7 +372,7 @@
             for copy in env_copies(k, c, lax.rem(c + k, n_col)):
                 copy.wait_send()
 
-    apply(1, theta_of, 2)
+    apply(1, theta_of, 3)
     for k in range(1, n_col):
         settle(own, z_send.at[k - 1])
 

time: 36.8 us -> 37.7 us (1.024)
  Pallas kernels: 34.3 us -> 35.3 us
    pallas_call x1, Pallas kernels: 34.3 us -> 35.3 us  [body(): pl.pallas_call(functools.partial(kernel, n_blk, n_col), out_shape=(out, o...]
where the time goes in v10:
time: 37.7 us; the launch traced here: 37.5 us
  Pallas kernels  35.3 us (94%)
  local copies, waits for them, and re-layouts  1.63 us (4%)
  between operations  0.64 us (2%)
    pallas_call x1, Pallas kernels, body(): pl.pallas_call(functools.partial(kernel, n_blk, n_col), out_shape=(out, o...  35.3 us
    unnamed x2, local copies, waits for them, and re-layouts  1.63 us

profile of v10, /device:TPU:7, one launch (start us, length us, event | category | flops | bytes accessed | tf_op | source)
XLA Modules:
  0.0 37.5 jit_solution(15281161156558556759)
XLA Ops:
  0.6 35.3 %shard_map.68 = (f32[2,192,384]{2,1,0:T(8,128)S(1)}, f32[2,192,384]{2,1,0:T(8,128)S(1)}) custom-call(s32[2]{0:T(128)} %dims_in.1, s32[2,5]{1,0:T(2,128)} %pattern_in.1, bf16[2,192,384]{2,1,0:T(8,128)(2,1)} %psi.1, bf16[2,2,384,384]{3,2,1,0:T(8,128)(2,1)} %left_env.1, bf16[2,384,384]{2,1,0:T(8,128)(2,1)} %right_env.1), custom_call_target="tpu_custom_call" | custom-call | tf_op jit(solution)/shard_map/pallas_call | solution.py:390
  35.9 0.8 %copy.9 = f32[2,192,384]{2,1,0:T(8,128)} copy(f32[2,192,384]{2,1,0:T(8,128)S(1)} %get-tuple-element.2) | data formatting | bytes 1179648
  36.7 0.8 %copy.10 = f32[2,192,384]{2,1,0:T(8,128)} copy(f32[2,192,384]{2,1,0:T(8,128)S(1)} %get-tuple-element.3) | data formatting | bytes 1179648

commit v11 on v9

--- a/solution.py
+++ b/solution.py
@@ -139,6 +139,16 @@
             device_id_type=MESH,
         )
 
+    first_core = lax.rem(c, 2) == 0
+
+    def start_halo(h):
+        to_pair(h, 0).start()
+
+        @pl.when(first_core)
+        def _():
+            for i in range(1, len(chunks)):
+                to_pair(h, i).start()
+
     def z_part(h, i, holder):
         p, r = chunks[i]
         start = pl.multiple_of(holder * rows + r * height, 16)
@@ -174,8 +184,7 @@
             )
         ]
 
-    for i in range(len(chunks)):
-        to_pair(0, i).start()
+    start_halo(0)
     for k in range(1, n_col):
         for copy in env_copies(k, c, lax.rem(c + k, n_col)):
             copy.start()
@@ -279,6 +288,13 @@
                 def _():
                     to_onward(h, i).start()
 
+                if i == 0:
+
+                    @pl.when(jnp.logical_not(first_core))
+                    def _():
+                        for m in range(1, count):
+                            to_pair(h, m).start()
+
                 combine_near(h, i)
                 if h == 0 and i == 1:
                     settle_env()
@@ -344,8 +360,7 @@
 
     for m in range(1, mates):
         stat_to_mate(m).start()
-    for i in range(len(chunks)):
-        to_pair(1, i).start()
+    start_halo(1)
     settle(stat_mate, stat_sem.at[1])
     stat_sum[...] = stat_own[...] + jnp.sum(stat_mate[...], axis=0)
 

time: 36.8 us -> 36.1 us (0.981)
  Pallas kernels: 34.3 us -> 33.6 us
    pallas_call x1, Pallas kernels: 34.3 us -> 33.6 us  [body(): pl.pallas_call(functools.partial(kernel, n_blk, n_col), out_shape=(out, o...]
where the time goes in v11:
time: 36.1 us; the launch traced here: 35.9 us
  Pallas kernels  33.6 us (93%)
  local copies, waits for them, and re-layouts  1.63 us (5%)
  between operations  0.64 us (2%)
    pallas_call x1, Pallas kernels, body(): pl.pallas_call(functools.partial(kernel, n_blk, n_col), out_shape=(out, o...  33.6 us
    unnamed x2, local copies, waits for them, and re-layouts  1.63 us

profile of v11, /device:TPU:7, one launch (start us, length us, event | category | flops | bytes accessed | tf_op | source)
XLA Modules:
  0.0 35.9 jit_solution(5952281823904483475)
XLA Ops:
  0.6 33.6 %shard_map.68 = (f32[2,192,384]{2,1,0:T(8,128)S(1)}, f32[2,192,384]{2,1,0:T(8,128)S(1)}) custom-call(s32[2]{0:T(128)} %dims_in.1, s32[2,5]{1,0:T(2,128)} %pattern_in.1, bf16[2,192,384]{2,1,0:T(8,128)(2,1)} %psi.1, bf16[2,2,384,384]{3,2,1,0:T(8,128)(2,1)} %left_env.1, bf16[2,384,384]{2,1,0:T(8,128)(2,1)} %right_env.1), custom_call_target="tpu_custom_call" | custom-call | tf_op jit(solution)/shard_map/pallas_call | solution.py:405
  34.2 0.8 %copy.9 = f32[2,192,384]{2,1,0:T(8,128)} copy(f32[2,192,384]{2,1,0:T(8,128)S(1)} %get-tuple-element.2) | data formatting | bytes 1179648
  35.0 0.8 %copy.10 = f32[2,192,384]{2,1,0:T(8,128)} copy(f32[2,192,384]{2,1,0:T(8,128)S(1)} %get-tuple-element.3) | data formatting | bytes 1179648

commit v12 on v11

--- a/solution.py
+++ b/solution.py
@@ -185,9 +185,13 @@
         ]
 
     start_halo(0)
-    for k in range(1, n_col):
-        for copy in env_copies(k, c, lax.rem(c + k, n_col)):
-            copy.start()
+
+    def start_env():
+        for k in range(1, n_col):
+            for copy in env_copies(k, c, lax.rem(c + k, n_col)):
+                copy.start()
+
+    pl.when(jnp.logical_not(first_core))(start_env)
 
     coeff = [[pattern[s, j].astype(jnp.float32) for j in range(5)] for s in range(2)]
     zero = jnp.float32(0.0)
@@ -295,8 +299,11 @@
                         for m in range(1, count):
                             to_pair(h, m).start()
 
+                    if h == 0:
+                        pl.when(first_core)(start_env)
+
                 combine_near(h, i)
-                if h == 0 and i == 1:
+                if h == 0 and i == 2 * HALVES:
                     settle_env()
 
             j = i - lag

time: 36.1 us -> 36.1 us (level)
  no operation moved by 1% of the time
where the time goes in v12:
time: 36.1 us; the launch traced here: 35.9 us
  Pallas kernels  33.6 us (93%)
  local copies, waits for them, and re-layouts  1.63 us (5%)
  between operations  0.64 us (2%)
    pallas_call x1, Pallas kernels, body(): pl.pallas_call(functools.partial(kernel, n_blk, n_col), out_shape=(out, o...  33.6 us
    unnamed x2, local copies, waits for them, and re-layouts  1.63 us

profile of v12, /device:TPU:7, one launch (start us, length us, event | category | flops | bytes accessed | tf_op | source)
XLA Modules:
  0.0 35.9 jit_solution(3851597094054989103)
XLA Ops:
  0.6 33.6 %shard_map.68 = (f32[2,192,384]{2,1,0:T(8,128)S(1)}, f32[2,192,384]{2,1,0:T(8,128)S(1)}) custom-call(s32[2]{0:T(128)} %dims_in.1, s32[2,5]{1,0:T(2,128)} %pattern_in.1, bf16[2,192,384]{2,1,0:T(8,128)(2,1)} %psi.1, bf16[2,2,384,384]{3,2,1,0:T(8,128)(2,1)} %left_env.1, bf16[2,384,384]{2,1,0:T(8,128)(2,1)} %right_env.1), custom_call_target="tpu_custom_call" | custom-call | tf_op jit(solution)/shard_map/pallas_call | solution.py:412
  34.2 0.8 %copy.9 = f32[2,192,384]{2,1,0:T(8,128)} copy(f32[2,192,384]{2,1,0:T(8,128)S(1)} %get-tuple-element.2) | data formatting | bytes 1179648
  35.0 0.8 %copy.10 = f32[2,192,384]{2,1,0:T(8,128)} copy(f32[2,192,384]{2,1,0:T(8,128)S(1)} %get-tuple-element.3) | data formatting | bytes 1179648

commit v13 on v12

--- a/solution.py
+++ b/solution.py
@@ -146,8 +146,7 @@
 
         @pl.when(first_core)
         def _():
-            for i in range(1, len(chunks)):
-                to_pair(h, i).start()
+            to_pair(h, 1).start()
 
     def z_part(h, i, holder):
         p, r = chunks[i]
@@ -292,15 +291,11 @@
                 def _():
                     to_onward(h, i).start()
 
-                if i == 0:
-
-                    @pl.when(jnp.logical_not(first_core))
-                    def _():
-                        for m in range(1, count):
-                            to_pair(h, m).start()
-
-                    if h == 0:
-                        pl.when(first_core)(start_env)
+                for core_is, ahead in ((first_core, 2), (jnp.logical_not(first_core), 1)):
+                    if i + ahead < count:
+                        pl.when(core_is)(to_pair(h, i + ahead).start)
+                if i == 0 and h == 0:
+                    pl.when(first_core)(start_env)
 
                 combine_near(h, i)
                 if h == 0 and i == 2 * HALVES:

time: 36.1 us -> 36.6 us (1.014)
  Pallas kernels: 33.6 us -> 34.2 us
    pallas_call x1, Pallas kernels: 33.6 us -> 34.2 us  [body(): pl.pallas_call(functools.partial(kernel, n_blk, n_col), out_shape=(out, o...]
where the time goes in v13:
time: 36.6 us; the launch traced here: 36.4 us
  Pallas kernels  34.2 us (93%)
  local copies, waits for them, and re-layouts  1.63 us (4%)
  between operations  0.64 us (2%)
    pallas_call x1, Pallas kernels, body(): pl.pallas_call(functools.partial(kernel, n_blk, n_col), out_shape=(out, o...  34.2 us
    unnamed x2, local copies, waits for them, and re-layouts  1.63 us

profile of v13, /device:TPU:7, one launch (start us, length us, event | category | flops | bytes accessed | tf_op | source)
XLA Modules:
  0.0 36.4 jit_solution(7273124052561568789)
XLA Ops:
  0.6 34.2 %shard_map.68 = (f32[2,192,384]{2,1,0:T(8,128)S(1)}, f32[2,192,384]{2,1,0:T(8,128)S(1)}) custom-call(s32[2]{0:T(128)} %dims_in.1, s32[2,5]{1,0:T(2,128)} %pattern_in.1, bf16[2,192,384]{2,1,0:T(8,128)(2,1)} %psi.1, bf16[2,2,384,384]{3,2,1,0:T(8,128)(2,1)} %left_env.1, bf16[2,384,384]{2,1,0:T(8,128)(2,1)} %right_env.1), custom_call_target="tpu_custom_call" | custom-call | tf_op jit(solution)/shard_map/pallas_call | solution.py:407
  34.8 0.8 %copy.9 = f32[2,192,384]{2,1,0:T(8,128)} copy(f32[2,192,384]{2,1,0:T(8,128)S(1)} %get-tuple-element.2) | data formatting | bytes 1179648
  35.6 0.8 %copy.10 = f32[2,192,384]{2,1,0:T(8,128)} copy(f32[2,192,384]{2,1,0:T(8,128)S(1)} %get-tuple-element.3) | data formatting | bytes 1179648
